TPU v7x, 256 devices: a whole 4x4x8 slice. The times are simulated.
256 devices in a mesh: section: 2 (over core), tensor: 32 (over x, z), dp: 4 (over y).
Axes of the slice: x: 4, y: 4, z: 8, core: 2. Of those that a mesh axis runs over, the one named last changes fastest.
Arguments:
- grad_out: bfloat16 [2, 4, 512, 6144], P('section', 'dp', 'tensor'), may hold values from -6 to 6
- drop_seed: int32 [2], P('section'), may hold values from 0 to 1048575
- layer_in: bfloat16 [2, 4, 512, 6144], P('section', 'dp', 'tensor')
- ln_gain: float32 [2, 6144], P('section'), may hold values from 0.1 to 1.9
- pre_act: bfloat16 [2, 4, 512, 24576], P('section', 'dp', None, 'tensor'), may hold values from -6 to 6
- fc1_weight: bfloat16 [2, 24576, 6144], P('section', 'tensor', 'dp'), may hold values from -0.078125 to 0.078125
- fc2_weight: bfloat16 [2, 6144, 24576], P('section', 'dp', 'tensor'), may hold values from -0.0390625 to 0.0390625
Outputs:
- arriving_grad: bfloat16 [2, 4, 512, 6144], P('section', 'dp', 'tensor')
- fc2_weight_grad: bfloat16 [2, 6144, 24576], P('section', 'dp', 'tensor')
All inputs are finite; a program needn't handle non-finite values.
Results may differ from a plain program's by a relative error of at most 0.013.
Values may be sent and summed in bfloat16 or wider, within the bound.
A program may use at most 128 MiB of HBM per device.

v0:
```python
import jax
import jax.numpy as jnp
from jax import lax
from jax.sharding import PartitionSpec as P

KEEP_SCALE = 1.0 / 0.9
NORM_EPS = 1e-05


def passed_along(value, axis, by):
    peers = lax.axis_size(axis)
    return lax.ppermute(value, axis, [(i, (i + by) % peers) for i in range(peers)])


def scramble(hashed):
    hashed = hashed * jnp.int32(739982445)
    hashed = hashed ^ jnp.right_shift(hashed, 15) & jnp.int32(131071)
    hashed = hashed * jnp.int32(695872825)
    hashed = hashed ^ jnp.right_shift(hashed, 13) & jnp.int32(524287)
    return hashed


def keep_table(seed_value, replica, first_row, row_count, feature_count):
    row_ids = first_row + lax.iota(jnp.int32, row_count)
    columns = lax.iota(jnp.int32, feature_count)
    offset = (seed_value * jnp.int32(131) + replica) * jnp.int32(1640531527)
    hashed = scramble(row_ids[:, None] * jnp.int32(feature_count) + columns[None, :] + offset)
    return jnp.right_shift(hashed, 9) & jnp.int32(1023) < jnp.int32(922)


def norm_back(upstream, normed_grad, layer_rows, gain):
    values = layer_rows.astype(jnp.float32)
    center = values - jnp.mean(values, axis=-1, keepdims=True)
    inv_std = lax.rsqrt(jnp.mean(center * center, axis=-1, keepdims=True) + NORM_EPS)
    x_hat = center * inv_std
    scaled = normed_grad * gain
    bracket = (
        scaled
        - jnp.mean(scaled, axis=-1, keepdims=True)
        - x_hat * jnp.mean(scaled * x_hat, axis=-1, keepdims=True)
    )
    return (upstream.astype(jnp.float32) + inv_std * bracket).astype(jnp.bfloat16)


def shards(grad_out, drop_seed, layer_in, ln_gain, pre_act, fc1_weight, fc2_weight):
    upstream = grad_out[0, 0]
    token_rows = upstream.shape[0]
    feature_count = upstream.shape[1]
    first_row = lax.axis_index("tensor") * token_rows
    kept_cells = keep_table(
        drop_seed[0], lax.axis_index("dp"), first_row, token_rows, feature_count
    )
    factor = jnp.where(kept_cells, jnp.float32(KEEP_SCALE), jnp.float32(0.0))
    branch_grad = (upstream.astype(jnp.float32) * factor).astype(jnp.bfloat16)
    pre_rows = pre_act[0, 0]
    w_in = fc1_weight[0]
    w_out = fc2_weight[0]
    gathered = lax.all_gather(branch_grad, "tensor", axis=0, tiled=True)
    columns = gathered
    hidden_grad = jnp.dot(
        columns, lax.all_gather(w_out, "dp", axis=0, tiled=True), preferred_element_type=jnp.float32
    )
    act_grad = jnp.where(pre_rows > 0, hidden_grad, jnp.float32(0.0)).astype(jnp.bfloat16)
    partial_sum = jnp.dot(
        act_grad, lax.all_gather(w_in, "dp", axis=1, tiled=True), preferred_element_type=jnp.float32
    )
    normed_grad = lax.psum_scatter(
        partial_sum.astype(jnp.bfloat16), "tensor", scatter_dimension=0, tiled=True
    ).astype(jnp.float32)
    hidden = jnp.maximum(pre_rows, 0)
    columns = gathered
    weight_grad = lax.psum_scatter(
        lax.dot_general(
            columns, hidden, (((0,), (0,)), ((), ())), preferred_element_type=jnp.float32
        ).astype(jnp.bfloat16),
        "dp",
        scatter_dimension=0,
        tiled=True,
    )
    input_grad = norm_back(upstream, normed_grad, layer_in[0, 0], ln_gain[0])
    arriving = passed_along(input_grad, "section", -1)
    return (arriving[None, None], weight_grad[None])


def solution(mesh):
    placed = (
        P("section", "dp", "tensor", None),
        P("section"),
        P("section", "dp", "tensor", None),
        P("section", None),
        P("section", "dp", None, "tensor"),
        P("section", "tensor", "dp"),
        P("section", "dp", "tensor"),
    )
    return jax.shard_map(
        shards,
        mesh=mesh,
        in_specs=placed,
        out_specs=(P("section", "dp", "tensor", None), P("section", "dp", "tensor")),
        check_vma=False,
    )
```

profile of v0, /device:TPU:1, one launch (start us, length us, event | category | flops | bytes accessed | tf_op | source)
XLA Modules:
  0.0 631.3 jit_solution(11345111322123795046)
XLA Ops:
  7.2 0.0 all-gather.6.cloned.1.call-start
  7.9 1.9 fusion.20
  9.7 0.0 all-gather.6.cloned.1.call-update
  9.8 0.0 all-gather.8.cloned.1.call-start
  9.8 0.7 all-gather.8.cloned.1.call-update
  10.5 0.0 all-gather.10.cloned.1.call-start
  10.6 0.7 all-gather.10.cloned.1.call-update
  11.3 0.0 reduce-scatter.3.cloned.1.call-start
  11.3 92.0 %all-gather.6.cloned.1.call-done = bf16[512,6144]{1,0:T(8,128)(2,1)} async-done(((bf16[16,6144]{1,0:T(8,128)(2,1)}), bf16[512,6144]{1,0:T(8,128)(2,1)}) %all-gather.6.cloned.1.call-update) | async-done | bytes 6291472 | tf_op jit(solution)/shard_map/all_gather | solution.py:58
  103.3 93.7 %all-gather.8.cloned.1.call-done = bf16[1,6144,768]{2,1,0:T(8,128)(2,1)} async-done(((bf16[1,1536,768]{2,1,0:T(8,128)(2,1)}), bf16[1,6144,768]{2,1,0:T(8,128)(2,1)}) %all-gather.8.cloned.1.call-update) | async-done | bytes 9437200 | tf_op jit(solution)/shard_map/all_gather | solution.py:61
  197.0 10.0 %select_convert_fusion = bf16[512,768]{1,0:T(8,128)(2,1)S(1)} fusion(bf16[1,1,512,768]{3,2,1,0:T(8,128)(2,1)} %param.11, bf16[512,6144]{1,0:T(8,128)(2,1)} %all-gather.6.cloned.1.call-done, bf16[1,6144,768]{2,1,0:T(8,128)(2,1)} %all-gather.8.cloned.1.call-done), kind=kOutput, calls=%fused_computation.6 | convolution fusion | flops 4833017856 | bytes 17301504 | tf_op jit(solution)/shard_map/dot_general | solution.py:60
  207.0 87.3 %all-gather.10.cloned.1.call-done = bf16[1,768,6144]{2,1,0:T(8,128)(2,1)} async-done(((bf16[1,768,1536]{2,1,0:T(8,128)(2,1)}), bf16[1,768,6144]{2,1,0:T(8,128)(2,1)}) %all-gather.10.cloned.1.call-update) | async-done | bytes 9437200 | tf_op jit(solution)/shard_map/all_gather | solution.py:65
  294.4 10.6 %fusion.4 = bf16[512,6144]{1,0:T(8,128)(2,1)} fusion(bf16[512,768]{1,0:T(8,128)(2,1)S(1)} %select_convert_fusion, bf16[1,768,6144]{2,1,0:T(8,128)(2,1)} %all-gather.10.cloned.1.call-done), kind=kOutput, calls=%fused_computation.5 | convolution fusion | flops 4834983936 | bytes 16515072 | tf_op jit(solution)/shard_map/dot_general | solution.py:64
  304.9 0.0 copy-start.3
  304.9 0.0 reduce-scatter.3.cloned.1.call-update
  305.0 0.0 reduce-scatter.5.cloned.1.call-start
  305.0 1.1 copy-done.3
  306.1 10.2 %convolution_convert_fusion = bf16[6144,768]{1,0:T(8,128)(2,1)} fusion(bf16[512,6144]{1,0:T(8,128)(2,1)} %all-gather.6.cloned.1.call-done, bf16[1,1,512,768]{3,2,1,0:T(8,128)(2,1)S(1)} %copy-done.3), kind=kOutput, calls=%fused_computation | convolution fusion | flops 4836950016 | bytes 16515072 | tf_op jit(solution)/shard_map/dot_general | solution.py:73
  316.3 0.0 copy-start
  316.3 0.0 copy-start.2
  316.3 0.0 copy-start.1
  316.3 0.0 reduce-scatter.5.cloned.1.call-update
  316.3 0.9 copy-done
  317.2 0.2 convert_reduce_fusion
  317.4 0.2 fusion.19
  317.6 209.3 %reduce-scatter.3.cloned.1.call-done = bf16[16,6144]{1,0:T(8,128)(2,1)} async-done(((bf16[512,6144]{1,0:T(8,128)(2,1)}), bf16[16,6144]{1,0:T(8,128)(2,1)}) %reduce-scatter.3.cloned.1.call-update) | async-done | bytes 196624 | tf_op jit(solution)/shard_map/reduce_scatter | solution.py:67
  526.9 0.0 copy-done.2
  526.9 1.2 fusion.22
  528.1 0.0 copy-done.1
  528.1 1.1 fusion.21
  529.3 4.7 collective-permute-start
  534.0 1.1 collective-permute-done
  535.0 89.0 %reduce-scatter.5.cloned.1.call-done = bf16[1536,768]{1,0:T(8,128)(2,1)} async-done(((bf16[6144,768]{1,0:T(8,128)(2,1)}), bf16[1536,768]{1,0:T(8,128)(2,1)}) %reduce-scatter.5.cloned.1.call-update) | async-done | bytes 2359312 | tf_op jit(solution)/shard_map/reduce_scatter | solution.py:72
  624.0 0.7 copy.11
  (4 shorter events, 0.0 us)
Async XLA Ops:
  7.2 96.1 %all-gather.6.cloned.1.call-start = ((), (), s32[]{:S(2)}) async-start(), calls=%async_computation.2 | async-start | bytes 6488064 | tf_op jit(solution)/shard_map/all_gather | solution.py:58
  9.8 187.3 %all-gather.8.cloned.1.call-start = ((), (), s32[]{:S(2)}) async-start(), calls=%async_computation.5 | async-start | bytes 11796480 | tf_op jit(solution)/shard_map/all_gather | solution.py:61
  10.5 283.9 %all-gather.10.cloned.1.call-start = ((), (), s32[]{:S(2)}) async-start(), calls=%async_computation.6 | async-start | bytes 11796480 | tf_op jit(solution)/shard_map/all_gather | solution.py:65
  11.3 515.7 %reduce-scatter.3.cloned.1.call-start = ((), (), s32[]{:S(2)}) async-start(), calls=%async_computation.3 | async-start | bytes 6488064 | tf_op jit(solution)/shard_map/reduce_scatter | solution.py:67
  304.9 1.1 copy-start.3
  305.0 319.1 %reduce-scatter.5.cloned.1.call-start = ((), (), s32[]{:S(2)}) async-start(), calls=%async_computation.4 | async-start | bytes 11796480 | tf_op jit(solution)/shard_map/reduce_scatter | solution.py:72
  316.3 0.9 copy-start
  316.3 210.6 %copy-start.2 = (f32[1,6144]{1,0:T(1,128)S(1)}, f32[1,6144]{1,0:T(1,128)}, u32[]{:S(2)}) copy-start(f32[1,6144]{1,0:T(1,128)} %param.10) | copy-start | bytes 73732
  316.3 211.8 %copy-start.1 = (bf16[1,1,16,6144]{3,2,1,0:T(8,128)(2,1)S(1)}, bf16[1,1,16,6144]{3,2,1,0:T(8,128)(2,1)}, u32[]{:S(2)}) copy-start(bf16[1,1,16,6144]{3,2,1,0:T(8,128)(2,1)} %param.7) | copy-start | bytes 589828
  529.3 5.8 collective-permute-start
Sparse Core Ops, SparseCore 0:
  11.1 92.0 all-gather.5
  105.1 91.8 all-gather.7
  198.8 95.4 all-gather.9
  305.1 221.7 reduce-scatter.2
  530.1 93.8 reduce-scatter.4
where the time goes:
time: 632 us; the launch traced here: 631 us
  waiting for transfers between devices  574 us (91%)
  matrix products  30.8 us (5%)
  between operations  14.5 us (2%)
    reduce_scatter x1, waiting for transfers between devices, shards(): lax.psum_scatter(partial_sum.astype(jnp.bfloat16), 'tensor', scatter_dime...  209 us
    all_gather x1, waiting for transfers between devices, shards(): lax.all_gather(w_out, 'dp', axis=0, tiled=True)  93.7 us
    all_gather x1, waiting for transfers between devices, shards(): gathered = lax.all_gather(branch_grad, 'tensor', axis=0, tiled=True)  92 us
    reduce_scatter x1, waiting for transfers between devices, shards(): lax.psum_scatter(lax.dot_general(columns, hidden, (((0,), (0,)), ((), ())...  89 us
    all_gather x1, waiting for transfers between devices, shards(): lax.all_gather(w_in, 'dp', axis=1, tiled=True)  87.3 us
  transfers between devices with their start and end apart: 6, of which 6 were waited for; matrix products, arithmetic and copies ran while one was open for 4% of the time, Pallas kernels for 0%

commit v1 on v0

v1 whole, which is shorter than its diff:
```python
import functools

import jax
import jax.numpy as jnp
from jax import lax
from jax.experimental import pallas as pl
from jax.experimental.pallas import tpu as pltpu
from jax.sharding import PartitionSpec as P

KEEP_SCALE = 1.0 / 0.9
NORM_EPS = 1e-05
MESH = pl.DeviceIdType.MESH
X, Z, Y = 4, 8, 4
BF, F32 = jnp.bfloat16, jnp.float32

AG_A, AG_B, YR, RS_A, RS_B, WG, HF, LN0 = range(8)


def default_order():
    order = [(HF, 0, 0)]
    for tick in range(7 + Y - 1):
        for m in range(Y):
            k = tick - m
            if 0 <= k < 7:
                order += [(AG_A, m, k), (AG_B, m, k)]
                if k == 6:
                    order += [(YR, m, 0)]
        if tick == 3:
            order += [(HF, 0, 1)]
    order += [(HF, 0, 2), (LN0, 0, 0)]
    fill = list(range(6))
    for tick in range(4 + Y - 1 + 7):
        for m in range(Y):
            k = tick - m
            if 0 <= k < 4:
                order += [(YR, m, k + 1)]
            if 4 <= k < 11:
                order += [(RS_A, m, k - 4), (RS_B, m, k - 4)]
        if fill:
            order += [(WG, fill.pop(0), 0)]
    return order


ORDER = default_order()


def scramble(hashed):
    hashed = hashed * jnp.int32(739982445)
    hashed = hashed ^ jnp.right_shift(hashed, 15) & jnp.int32(131071)
    hashed = hashed * jnp.int32(695872825)
    hashed = hashed ^ jnp.right_shift(hashed, 13) & jnp.int32(524287)
    return hashed


def kernel(
    cols_a, seed_ref, grad_ref, layer_ref, gain_ref, pre_hbm, w1_hbm, w2_hbm,
    out_hbm, wg_hbm,
    branch, G, H, W1, W2, PH, RY1, RY2, ACT, N, RA4, RA, RAX2, RAX1, RB2, RB1, RBZ4, RBZ,
    WGR, xhat, inv, final, result, ssem, rsem, lsem,
):
    s = lax.axis_index("section")
    t = lax.axis_index("tensor")
    q = lax.axis_index("dp")
    x, z = t // Z, t % Z
    rows = grad_ref.shape[0]
    width = grad_ref.shape[1]
    block = width // Y
    hidden_cols = H.shape[-1]
    tok = H.shape[1]
    shard = tok // Y
    half = shard // 2
    A, B = pl.ds(0, cols_a), pl.ds(cols_a, block - cols_a)

    def xi(d):
        return (x + d + X) % X

    def zi(d):
        return (z + d + Z) % Z

    def yi(d):
        return (q + d + Y) % Y

    to = {
        "x+": (s, xi(1) * Z + z, q),
        "x-": (s, xi(-1) * Z + z, q),
        "z+": (s, x * Z + zi(1), q),
        "z-": (s, x * Z + zi(-1), q),
        "y+": (s, t, yi(1)),
        "y-": (s, t, yi(-1)),
        "y2": (s, t, yi(2)),
        "c": (1 - s, t, q),
    }
    copies = []
    pending = []

    def send(src, dst, where):
        i = len(copies)
        c = pltpu.make_async_remote_copy(
            src_ref=src, dst_ref=dst, send_sem=ssem.at[i], recv_sem=rsem.at[i],
            device_id=to[where], device_id_type=MESH,
        )
        copies.append(c)
        pending.append(c)
        c.start()
        return c

    def drain():
        for c in pending:
            c.wait_send()
        pending.clear()

    load_pre = pltpu.make_async_copy(pre_hbm, H.at[q], lsem.at[0])
    load_w2 = pltpu.make_async_copy(w2_hbm, W2, lsem.at[1])
    load_w1 = pltpu.make_async_copy(w1_hbm, W1, lsem.at[2])
    load_pre.start()
    load_w2.start()
    load_w1.start()

    barrier = pltpu.get_barrier_semaphore()
    for where in to.values():
        pl.semaphore_signal(barrier, inc=1, device_id=where, device_id_type=MESH)

    offset = (seed_ref[0] * jnp.int32(131) + q) * jnp.int32(1640531527)
    row_ids = t * rows + lax.broadcasted_iota(jnp.int32, (rows, block), 0)
    col_ids = lax.broadcasted_iota(jnp.int32, (rows, block), 1)
    base = row_ids * jnp.int32(width) + col_ids + offset
    for j in range(Y):
        hashed = scramble(base + jnp.int32(j * block))
        kept = (jnp.right_shift(hashed, 9) & jnp.int32(1023)) < jnp.int32(922)
        factor = jnp.where(kept, F32(KEEP_SCALE), F32(0.0))
        branch[j] = (grad_ref[:, j * block:(j + 1) * block].astype(F32) * factor).astype(BF)

    pl.semaphore_wait(barrier, len(to))

    first = []
    for d, where in ((1, "y+"), (3, "y-"), (2, "y2")):
        first.append(send(branch.at[yi(d)], G.at[q, x, z], where))
    G[q, x, z] = branch[q]
    load_pre.wait()
    H[q] = jnp.maximum(H[q], jnp.zeros((), BF))

    st = {}

    def hidden_step(k):
        if k == 0:
            st["h1"] = (send(H.at[q], H.at[q], "y+"), send(H.at[q], H.at[q], "y-"))
        elif k == 1:
            p, n = st["h1"]
            lo, hi = pl.ds(0, tok // 2), pl.ds(tok // 2, tok // 2)
            p.wait_recv()
            c0 = send(H.at[yi(-1), lo], H.at[yi(-1), lo], "y+")
            n.wait_recv()
            c1 = send(H.at[yi(1), hi], H.at[yi(1), hi], "y-")
            st["h2"] = (c0, c1)
        else:
            for c in st["h2"]:
                c.wait_recv()

    def wait2(key):
        for c in st.pop(key):
            c.wait_recv()

    def same(ref, where):
        return send(ref, ref, where)

    def ag_a(m, k):
        key = ("aga", m)
        if k > 0:
            wait2(key)
        if k == 0:
            own = G.at[m, x, z, :, A]
            st[key] = (same(own, "x+"), same(own, "x-"))
        elif k == 1:
            if m % 2 == 0:
                st[key] = (same(G.at[m, xi(-1), z, :, A], "x+"),)
            else:
                st[key] = (same(G.at[m, xi(1), z, :, A], "x-"),)
        elif k < 5:
            d = k - 2
            st[key] = (
                same(G.at[m, :, zi(-d), :, A], "z+"),
                same(G.at[m, :, zi(d), :, A], "z-"),
            )
        elif k == 5:
            st[key] = (
                same(G.at[m, pl.ds(0, 2), zi(-3), :, A], "z+"),
                same(G.at[m, pl.ds(2, 2), zi(3), :, A], "z-"),
            )

    def ag_b(m, k):
        key = ("agb", m)
        if k > 0:
            wait2(key)
        if k < 3:
            st[key] = (
                same(G.at[m, x, zi(-k), :, B], "z+"),
                same(G.at[m, x, zi(k), :, B], "z-"),
            )
        elif k == 3:
            if m % 2 == 0:
                st[key] = (same(G.at[m, x, zi(-3), :, B], "z+"),)
            else:
                st[key] = (same(G.at[m, x, zi(3), :, B], "z-"),)
        elif k == 4:
            own = G.at[m, x, :, :, B]
            st[key] = (same(own, "x+"), same(own, "x-"))
        elif k == 5:
            st[key] = (
                same(G.at[m, xi(-1), pl.ds(0, 4), :, B], "x+"),
                same(G.at[m, xi(1), pl.ds(4, 4), :, B], "x-"),
            )

    def y_step(m, k):
        key = ("y", m)
        if k > 0:
            wait2(key)
        lo, hi = pl.ds(0, half), pl.ds(half, half)
        if k == 0:
            if m == 0:
                load_w2.wait()
            tile = 256

            @pl.loop(0, hidden_cols // tile)
            def _(n):
                cols = pl.ds(pl.multiple_of(n * tile, tile), tile)
                part = jnp.dot(
                    G[m].reshape(tok, block), W2[:, cols], preferred_element_type=F32
                )
                PH[m, :, :, cols] = part.astype(BF).reshape(Y, shard, tile)

            st[key] = (
                send(PH.at[m, yi(2), lo], RY1.at[m, 0], "y+"),
                send(PH.at[m, yi(2), hi], RY1.at[m, 1], "y-"),
            )
        elif k == 1:
            PH[m, yi(1), lo] = (PH[m, yi(1), lo].astype(F32) + RY1[m, 0].astype(F32)).astype(BF)
            PH[m, yi(-1), hi] = (PH[m, yi(-1), hi].astype(F32) + RY1[m, 1].astype(F32)).astype(BF)
            st[key] = (
                send(PH.at[m, yi(1)], RY2.at[m, 0], "y+"),
                send(PH.at[m, yi(-1)], RY2.at[m, 1], "y-"),
            )
        elif k == 2:
            total = PH[m, q].astype(F32) + RY2[m, 0].astype(F32) + RY2[m, 1].astype(F32)
            mine = pl.ds(pl.multiple_of(q * shard, shard), shard)
            ACT[m, q] = jnp.where(H[m, mine].astype(F32) > 0, total, F32(0.0)).astype(BF)
            st[key] = (same(ACT.at[m, q], "y+"), same(ACT.at[m, q], "y-"))
        elif k == 3:
            st[key] = (
                same(ACT.at[m, yi(-1), lo], "y+"),
                same(ACT.at[m, yi(1), hi], "y-"),
            )
        elif k == 4:
            if m == 0:
                load_w1.wait()
            tile = 256

            @pl.loop(0, block // tile)
            def _(n):
                cols = pl.ds(pl.multiple_of(n * tile, tile), tile)
                part = jnp.dot(
                    ACT[m].reshape(tok, hidden_cols), W1[:, cols], preferred_element_type=F32
                )
                N[m, :, :, :, cols] = part.astype(BF).reshape(X, Z, rows, tile)

    def add(index, received):
        N[index] = (N[index].astype(F32) + received.astype(F32)).astype(BF)

    def rs_a(m, k):
        key = ("rsa", m)
        if k > 0:
            wait2(key)
        lo, hi = pl.ds(0, 2), pl.ds(2, 2)
        if k == 0:
            st[key] = (
                send(N.at[m, lo, zi(4), :, A], RA4.at[m, 0], "z+"),
                send(N.at[m, hi, zi(4), :, A], RA4.at[m, 1], "z-"),
            )
        elif k < 4:
            d = 4 - k
            if k == 1:
                add((m, lo, zi(3), slice(None), A), RA4[m, 0])
                add((m, hi, zi(-3), slice(None), A), RA4[m, 1])
            else:
                add((m, slice(None), zi(d), slice(None), A), RA[m, 0, d])
                add((m, slice(None), zi(-d), slice(None), A), RA[m, 1, d])
            st[key] = (
                send(N.at[m, :, zi(d), :, A], RA.at[m, 0, d - 1], "z+"),
                send(N.at[m, :, zi(-d), :, A], RA.at[m, 1, d - 1], "z-"),
            )
        elif k == 4:
            index = (m, slice(None), z, slice(None), A)
            N[index] = (
                N[index].astype(F32) + RA[m, 0, 0].astype(F32) + RA[m, 1, 0].astype(F32)
            ).astype(BF)
            st[key] = (
                send(N.at[m, xi(2), z, :, A], RAX2.at[m], "x+" if m % 2 == 0 else "x-"),
            )
        elif k == 5:
            far = xi(1) if m % 2 == 0 else xi(-1)
            add((m, far, z, slice(None), A), RAX2[m])
            st[key] = (
                send(N.at[m, xi(1), z, :, A], RAX1.at[m, 0], "x+"),
                send(N.at[m, xi(-1), z, :, A], RAX1.at[m, 1], "x-"),
            )
        else:
            index = (m, x, z, slice(None), A)
            N[index] = (
                N[index].astype(F32) + RAX1[m, 0].astype(F32) + RAX1[m, 1].astype(F32)
            ).astype(BF)

    def rs_b(m, k):
        key = ("rsb", m)
        if k > 0:
            wait2(key)
        lo, hi = pl.ds(0, 4), pl.ds(4, 4)
        every = slice(None)
        if k == 0:
            st[key] = (
                send(N.at[m, xi(2), lo, :, B], RB2.at[m, 0], "x+"),
                send(N.at[m, xi(2), hi, :, B], RB2.at[m, 1], "x-"),
            )
        elif k == 1:
            add((m, xi(1), lo, every, B), RB2[m, 0])
            add((m, xi(-1), hi, every, B), RB2[m, 1])
            st[key] = (
                send(N.at[m, xi(1), :, :, B], RB1.at[m, 0], "x+"),
                send(N.at[m, xi(-1), :, :, B], RB1.at[m, 1], "x-"),
            )
        elif k == 2:
            index = (m, x, every, every, B)
            N[index] = (
                N[index].astype(F32) + RB1[m, 0].astype(F32) + RB1[m, 1].astype(F32)
            ).astype(BF)
            st[key] = (
                send(N.at[m, x, zi(4), :, B], RBZ4.at[m], "z+" if m % 2 == 0 else "z-"),
            )
        elif k < 6:
            d = 6 - k
            if k == 3:
                add((m, x, zi(3) if m % 2 == 0 else zi(-3), every, B), RBZ4[m])
            else:
                add((m, x, zi(d), every, B), RBZ[m, 0, d])
                add((m, x, zi(-d), every, B), RBZ[m, 1, d])
            st[key] = (
                send(N.at[m, x, zi(d), :, B], RBZ.at[m, 0, d - 1], "z+"),
                send(N.at[m, x, zi(-d), :, B], RBZ.at[m, 1, d - 1], "z-"),
            )
        else:
            index = (m, x, z, every, B)
            N[index] = (
                N[index].astype(F32) + RBZ[m, 0, 0].astype(F32) + RBZ[m, 1, 0].astype(F32)
            ).astype(BF)

    def weight_grad(j):
        tile = 256
        cols = pl.ds(j * tile, tile)
        left = G[:, :, :, :, cols].reshape(Y * tok, tile)
        part = lax.dot_general(
            left, H[...].reshape(Y * tok, hidden_cols), (((0,), (0,)), ((), ())),
            preferred_element_type=F32,
        )
        WGR[cols] = part.astype(BF)
        c = pltpu.make_async_copy(WGR.at[cols], wg_hbm.at[cols], lsem.at[3 + j])
        c.start()
        outs.append(c)

    outs = []

    def norm_stats():
        values = layer_ref[...].astype(F32)
        center = values - jnp.mean(values, axis=-1, keepdims=True)
        scale = lax.rsqrt(jnp.mean(center * center, axis=-1, keepdims=True) + NORM_EPS)
        xhat[...] = center * scale
        inv[...] = jnp.broadcast_to(scale, inv.shape)

    for c in first:
        c.wait_recv()

    for kind, m, k in ORDER:
        if kind == AG_A:
            ag_a(m, k)
        elif kind == AG_B:
            ag_b(m, k)
        elif kind == YR:
            if m == Y - 1 and k == 4:
                drain()
            y_step(m, k)
        elif kind == RS_A:
            rs_a(m, k)
        elif kind == RS_B:
            rs_b(m, k)
        elif kind == WG:
            weight_grad(m)
        elif kind == HF:
            hidden_step(k)
        else:
            norm_stats()

    last = []
    for d, where in ((1, "y+"), (3, "y-"), (2, "y2")):
        last.append(send(N.at[yi(d), x, z], final.at[q], where))
    final[q] = N[q, x, z]
    for c in outs:
        c.wait()
    for c in last:
        c.wait_recv()

    scale = inv[:, 0:1]
    total = jnp.zeros((rows, 1), F32)
    dotted = jnp.zeros((rows, 1), F32)
    for j in range(Y):
        cols = slice(j * block, (j + 1) * block)
        scaled = final[j].astype(F32) * gain_ref[:, cols]
        total += jnp.sum(scaled, axis=-1, keepdims=True)
        dotted += jnp.sum(scaled * xhat[:, cols], axis=-1, keepdims=True)
    total = total / width
    dotted = dotted / width
    for j in range(Y):
        cols = slice(j * block, (j + 1) * block)
        scaled = final[j].astype(F32) * gain_ref[:, cols]
        bracket = scaled - total - xhat[:, cols] * dotted
        result[:, cols] = (grad_ref[:, cols].astype(F32) + scale * bracket).astype(BF)
    done = send(result, out_hbm, "c")
    done.wait_recv()
    drain()


COPIES = 8 + 3 * 2 + 1 + Y * (11 + 13 + 8 + 13 + 11) + 8


def shards(grad_out, drop_seed, layer_in, ln_gain, pre_act, fc1_weight, fc2_weight):
    rows, width = grad_out.shape[2:]
    tok, hidden = pre_act.shape[2:]
    block = width // Y
    a = (block * 5 // 12) // 128 * 128
    b = block - a
    shard = tok // Y
    vmem = pl.BlockSpec(memory_space=pltpu.VMEM)
    anyspace = pl.BlockSpec(memory_space=pl.ANY)
    arriving, weight_grad = pl.pallas_call(
        functools.partial(kernel, a),
        out_shape=(
            jax.ShapeDtypeStruct((rows, width), BF),
            jax.ShapeDtypeStruct((block, hidden), BF),
        ),
        in_specs=[pl.BlockSpec(memory_space=pltpu.SMEM), vmem, vmem, vmem] + [anyspace] * 3,
        out_specs=(anyspace, anyspace),
        scratch_shapes=[
            pltpu.VMEM((Y, rows, block), BF),
            pltpu.VMEM((Y, X, Z, rows, block), BF),
            pltpu.VMEM((Y, tok, hidden), BF),
            pltpu.VMEM((hidden, block), BF),
            pltpu.VMEM((block, hidden), BF),
            pltpu.VMEM((Y, Y, shard, hidden), BF),
            pltpu.VMEM((Y, 2, shard // 2, hidden), BF),
            pltpu.VMEM((Y, 2, shard, hidden), BF),
            pltpu.VMEM((Y, Y, shard, hidden), BF),
            pltpu.VMEM((Y, X, Z, rows, block), BF),
            pltpu.VMEM((Y, 2, X // 2, rows, a), BF),
            pltpu.VMEM((Y, 2, 3, X, rows, a), BF),
            pltpu.VMEM((Y, rows, a), BF),
            pltpu.VMEM((Y, 2, rows, a), BF),
            pltpu.VMEM((Y, 2, Z // 2, rows, b), BF),
            pltpu.VMEM((Y, 2, Z, rows, b), BF),
            pltpu.VMEM((Y, rows, b), BF),
            pltpu.VMEM((Y, 2, 3, rows, b), BF),
            pltpu.VMEM((block, hidden), BF),
            pltpu.VMEM((rows, width), F32),
            pltpu.VMEM((rows, 128), F32),
            pltpu.VMEM((Y, rows, block), BF),
            pltpu.VMEM((rows, width), BF),
            pltpu.SemaphoreType.DMA((COPIES,)),
            pltpu.SemaphoreType.DMA((COPIES,)),
            pltpu.SemaphoreType.DMA((12,)),
        ],
        compiler_params=pltpu.CompilerParams(
            collective_id=0, has_side_effects=True, vmem_limit_bytes=60 * 1024 * 1024
        ),
    )(
        drop_seed, grad_out[0, 0], layer_in[0, 0], ln_gain,
        pre_act[0, 0], fc1_weight[0], fc2_weight[0],
    )
    return (arriving[None, None], weight_grad[None])


def solution(mesh):
    placed = (
        P("section", "dp", "tensor", None),
        P("section"),
        P("section", "dp", "tensor", None),
        P("section", None),
        P("section", "dp", None, "tensor"),
        P("section", "tensor", "dp"),
        P("section", "dp", "tensor"),
    )
    return jax.shard_map(
        shards,
        mesh=mesh,
        in_specs=placed,
        out_specs=(P("section", "dp", "tensor", None), P("section", "dp", "tensor")),
        check_vma=False,
    )
```

time: 632 us -> 176 us (0.28)
  waiting for transfers between devices: 574 us -> 0 us
  Pallas kernels: 0 us -> 170 us
  matrix products: 30.8 us -> 0 us
  between operations: 14.5 us -> 1.29 us
    reduce_scatter x2 -> x0, waiting for transfers between devices: 298 us -> none  [the longest x1 209 us: shards(): lax.psum_scatter(partial_sum.astype(jnp.bfloat16), 'tensor', scatter_dime...]
    all_gather x3 -> x0, waiting for transfers between devices: 273 us -> none  [the longest x1 93.7 us: shards(): lax.all_gather(w_out, 'dp', axis=0, tiled=True)]
    pallas_call x0 -> x1, Pallas kernels: none -> 170 us  [shards(): pl.pallas_call(functools.partial(kernel, a), out_shape=(jax.ShapeDtypeStr...]
    dot_general x3 -> x0, matrix products: 30.8 us -> none  [the longest x1 10.6 us: shards(): jnp.dot(act_grad, lax.all_gather(w_in, 'dp', axis=1, tiled=True), preferr...]
  transfers between devices with their start and end apart: 6 -> 0, of which waited for: 6 -> 0; matrix products, arithmetic and copies ran while one was open for 4% -> 0% of each run, Pallas kernels for 0% -> 0%
where the time goes in v1:
time: 176 us
  Pallas kernels  170 us (97%)
  local copies, waits for them, and re-layouts  4.84 us (3%)
    pallas_call x1, Pallas kernels, shards(): pl.pallas_call(functools.partial(kernel, a), out_shape=(jax.ShapeDtypeStr...  170 us
    unnamed x2, local copies, waits for them, and re-layouts  4.84 us

profile of v1, /device:TPU:1, one launch (start us, length us, event | category | flops | bytes accessed | tf_op | source)
XLA Modules:
  0.0 176.3 jit_solution(4073826458160494653)
XLA Ops:
  1.3 170.2 %shard_map.86 = (bf16[16,6144]{1,0:T(8,128)(2,1)}, bf16[1536,768]{1,0:T(8,128)(2,1)}) custom-call(s32[1]{0:T(128)S(6)} %copy.11.seed_ref, bf16[16,6144]{1,0:T(8,128)(2,1)} %bitcast.11, bf16[16,6144]{1,0:T(8,128)(2,1)} %bitcast.12, f32[1,6144]{1,0:T(1,128)} %gain_ref.1, bf16[512,768]{1,0:T(8,128)(2,1)} %bitcast.10, bf16[768,1536]{1,0:T(8,128)(2,1)} %bitcast.7, ...), custom_call_target="tpu_custom_call" | custom-call | tf_op jit(solution)/shard_map/pallas_call | solution.py:440
  171.5 1.6 copy.12
  173.1 3.2 %copy.13 = bf16[1,1536,768]{2,1,0:T(8,128)(2,1)} copy(bf16[1,1536,768]{2,1,0:T(8,128)(2,1)} %bitcast.9) | data formatting | bytes 4718592

commit v2 on v1

v2 whole, which is shorter than its diff:
```python
import functools

import jax
import jax.numpy as jnp
from jax import lax
from jax.experimental import pallas as pl
from jax.experimental.pallas import tpu as pltpu
from jax.sharding import PartitionSpec as P

KEEP_SCALE = 1.0 / 0.9
NORM_EPS = 1e-05
MESH = pl.DeviceIdType.MESH
X, Z, Y = 4, 8, 4
BF, F32 = jnp.bfloat16, jnp.float32

AG_A, AG_B, Y_LO, RS_A, RS_B, WG, HF, Y_HI, MM = range(9)


ORDER = (
    (1, 0, 0), (1, 2, 0), (0, 0, 0), (6, 0, 0), (1, 1, 0), (1, 0, 1), (0, 0, 1), (1, 2, 1), (0,
    3, 0), (1, 1, 1), (1, 0, 2), (0, 2, 0), (0, 0, 2), (1, 0, 3), (1, 3, 0), (0, 2, 1), (1, 2,
    2), (0, 0, 3), (0, 3, 1), (0, 2, 2), (1, 0, 4), (0, 0, 4), (0, 2, 3), (1, 2, 3), (1, 1, 2),
    (1, 3, 1), (0, 1, 0), (0, 0, 5), (0, 3, 2), (1, 0, 5), (1, 2, 4), (1, 3, 2), (6, 0, 1), (0,
    2, 4), (0, 1, 1), (0, 0, 6), (1, 0, 6), (2, 0, 0), (7, 0, 0), (1, 3, 3), (6, 0, 2), (2, 0,
    1), (0, 2, 5), (1, 2, 5), (0, 3, 3), (7, 0, 1), (2, 0, 2), (1, 3, 4), (0, 3, 4), (0, 2, 6),
    (1, 2, 6), (2, 2, 0), (7, 0, 2), (0, 1, 2), (7, 2, 0), (2, 2, 1), (0, 3, 5), (2, 0, 3), (1,
    3, 5), (0, 1, 3), (1, 1, 3), (7, 0, 3), (7, 2, 1), (0, 3, 6), (1, 1, 4), (2, 2, 2), (1, 3,
    6), (7, 3, 0), (2, 3, 0), (0, 1, 4), (8, 0, 4), (7, 2, 2), (4, 0, 0), (3, 0, 0), (7, 3, 1),
    (2, 2, 3), (1, 1, 5), (7, 2, 3), (0, 1, 5), (2, 3, 1), (4, 0, 1), (3, 0, 1), (7, 3, 2), (1,
    1, 6), (8, 2, 4), (0, 1, 6), (4, 2, 0), (3, 0, 2), (2, 3, 2), (7, 1, 0), (3, 2, 0), (7, 3,
    3), (2, 1, 0), (2, 3, 3), (4, 0, 2), (4, 2, 1), (7, 1, 1), (2, 1, 1), (8, 3, 4), (4, 3, 0),
    (4, 0, 3), (3, 2, 1), (3, 3, 0), (3, 0, 3), (7, 1, 2), (4, 0, 4), (2, 1, 2), (3, 2, 2), (3,
    3, 1), (4, 3, 1), (7, 1, 3), (3, 0, 4), (2, 1, 3), (4, 2, 2), (3, 2, 3), (6, 0, 3), (8, 1,
    4), (4, 1, 0), (3, 1, 0), (3, 3, 2), (3, 1, 1), (4, 2, 3), (4, 3, 2), (4, 1, 1), (4, 0, 5),
    (3, 3, 3), (3, 1, 2), (6, 0, 4), (5, 1, 0), (5, 2, 0), (3, 2, 4), (4, 2, 4), (4, 3, 3), (5,
    5, 0), (4, 1, 2), (3, 1, 3), (5, 4, 0), (3, 3, 4), (4, 1, 3), (5, 3, 0), (4, 3, 4), (3, 1,
    4), (3, 3, 5), (3, 0, 5), (4, 0, 6), (4, 1, 4), (4, 2, 5), (5, 0, 0), (4, 3, 5), (3, 1, 5),
    (4, 1, 5), (3, 2, 5), (4, 3, 6), (3, 0, 6), (4, 2, 6), (3, 3, 6), (3, 2, 6), (3, 1, 6), (4,
    1, 6),
)


def scramble(hashed):
    hashed = hashed * jnp.int32(739982445)
    hashed = hashed ^ jnp.right_shift(hashed, 15) & jnp.int32(131071)
    hashed = hashed * jnp.int32(695872825)
    hashed = hashed ^ jnp.right_shift(hashed, 13) & jnp.int32(524287)
    return hashed


def kernel(
    cols_a, cut, early, seed_ref, grad_hbm, layer_hbm, gain_hbm, pre_hbm, w1_hbm, w2_hbm,
    final, grad_out, layer_out, gain_out, wg_hbm,
    grad_ref, branch, G, H, W1, W2, PH, RY1A, RY2A, RY1B, RY2B, ACT, N, RA4, RA, RAX2, RAX1, RB2, RB1, RBZ4, RBZ,
    WGR, ssem, rsem, lsem,
):
    s = lax.axis_index("section")
    t = lax.axis_index("tensor")
    q = lax.axis_index("dp")
    x, z = t // Z, t % Z
    rows = grad_ref.shape[0]
    width = grad_ref.shape[1]
    block = width // Y
    hidden_cols = H.shape[-1]
    tok = H.shape[1]
    shard = tok // Y
    half = shard // 2
    A, B = pl.ds(0, cols_a), pl.ds(cols_a, block - cols_a)

    def xi(d):
        return (x + d + X) % X

    def zi(d):
        return (z + d + Z) % Z

    def yi(d):
        return (q + d + Y) % Y

    to = {
        "x+": (s, xi(1) * Z + z, q),
        "x-": (s, xi(-1) * Z + z, q),
        "z+": (s, x * Z + zi(1), q),
        "z-": (s, x * Z + zi(-1), q),
        "y+": (s, t, yi(1)),
        "y-": (s, t, yi(-1)),
        "y2": (s, t, yi(2)),
        "c": (1 - s, t, q),
        "cy+": (1 - s, t, yi(1)),
        "cy-": (1 - s, t, yi(-1)),
        "cy2": (1 - s, t, yi(2)),
    }
    count = [0]
    pending = {}

    def send(*parts, whole=None):
        i = count[0]
        count[0] += 1
        slot = i % SLOTS
        if slot in pending:
            pending.pop(slot).wait_send()

        def copy(src, dst, where):
            return pltpu.make_async_remote_copy(
                src_ref=src, dst_ref=dst, send_sem=ssem.at[slot], recv_sem=rsem.at[i],
                device_id=to[where], device_id_type=MESH,
            )

        for part in parts:
            started = copy(*part)
            started.start()
        pending[slot] = started if whole is None else copy(whole, whole, parts[0][2])
        return (pending[slot],)

    def drain():
        for c in pending.values():
            c.wait_send()
        pending.clear()

    with jax.named_scope("start"):
        barrier = pltpu.get_barrier_semaphore()
        for where in to.values():
            pl.semaphore_signal(barrier, inc=1, device_id=where, device_id_type=MESH)
        load_grad = pltpu.make_async_copy(grad_hbm, grad_ref, lsem.at[9])
        load_grad.start()
        load_pre = pltpu.make_async_copy(pre_hbm, H.at[q], lsem.at[0])
        load_w2 = pltpu.make_async_copy(w2_hbm, W2, lsem.at[1])
        load_w1 = pltpu.make_async_copy(w1_hbm, W1, lsem.at[2])
        load_pre.start()
        load_w2.start()
        load_w1.start()
        load_grad.wait()

        offset = (seed_ref[0] * jnp.int32(131) + q) * jnp.int32(1640531527)
        row_ids = t * rows + lax.broadcasted_iota(jnp.int32, (rows, block), 0)
        col_ids = lax.broadcasted_iota(jnp.int32, (rows, block), 1)
        base = row_ids * jnp.int32(width) + col_ids + offset
        for j in range(Y):
            hashed = scramble(base + jnp.int32(j * block))
            kept = (jnp.right_shift(hashed, 9) & jnp.int32(1023)) < jnp.int32(922)
            factor = jnp.where(kept, F32(KEEP_SCALE), F32(0.0))
            branch[j] = (grad_ref[:, j * block:(j + 1) * block].astype(F32) * factor).astype(BF)
        G[q, x, z] = branch[q]
        load_pre.wait()
        H[q] = jnp.maximum(H[q], jnp.zeros((), BF))

    with jax.named_scope("barrier"):
        pl.semaphore_wait(barrier, len(to))

    first = []
    for d, where in ((1, "y+"), (3, "y-"), (2, "y2")):
        first += send((branch.at[yi(d)], G.at[q, x, z], where))
    shared = []
    for src, dst in ((grad_hbm, grad_out), (layer_hbm, layer_out), (gain_hbm, gain_out)):
        shared += send((src, dst, "c"))

    st = {}

    def hidden_step(k):
        def piece(mb, part, rows_from, rows_count):
            return H.at[mb, pl.ds(pl.multiple_of(part * shard + rows_from, half), rows_count)]

        if k == 0:
            st["h1"] = same(H.at[q], "y+", H.at[q], "y-", whole=H.at[pl.ds(0, 2)])
        elif k == 1:
            wait2("h1")
            st["h2"] = same(
                piece(yi(-1), yi(1), 0, half), "y+", piece(yi(1), yi(-1), half, half), "y-",
                whole=H.at[0, pl.ds(0, shard)],
            )
        elif k == 2:
            wait2("h2")
        elif k == 3:
            st["h3"] = same(
                piece(yi(-1), yi(2), 0, shard), "y+", piece(yi(1), yi(2), 0, shard), "y-",
                whole=H.at[0, pl.ds(0, 2 * shard)],
            ) + same(
                piece(yi(-1), yi(3), 0, half), "y+", piece(yi(1), yi(1), half, half), "y-",
                whole=H.at[0, pl.ds(0, shard)],
            )
        else:
            wait2("h3")

    def wait2(key):
        for c in st.pop(key):
            c.wait_recv()

    def same(ref, where, other=None, other_where=None, whole=None):
        if other is None:
            return send((ref, ref, where))
        return send((ref, ref, where), (other, other, other_where), whole=whole)

    def ag_a(m, k):
        key = ("aga", m)
        if k > 0:
            wait2(key)
        if k == 0:
            own = G.at[m, x, z, :, A]
            st[key] = same(own, "x+", own, "x-", whole=RAX1.at[m])
        elif k == 1:
            if m % 2 == 0:
                st[key] = same(G.at[m, xi(-1), z, :, A], "x+")
            else:
                st[key] = same(G.at[m, xi(1), z, :, A], "x-")
        elif k < 5:
            d = k - 2
            st[key] = same(
                G.at[m, :, zi(-d), :, A], "z+", G.at[m, :, zi(d), :, A], "z-", whole=RA.at[m, :, 0]
            )
        elif k == 5:
            st[key] = same(
                G.at[m, pl.ds(0, 2), zi(-3), :, A], "z+", G.at[m, pl.ds(2, 2), zi(3), :, A], "z-",
                whole=RA4.at[m],
            )

    def ag_b(m, k):
        key = ("agb", m)
        if k > 0:
            wait2(key)
        if k < 3:
            st[key] = same(
                G.at[m, x, zi(-k), :, B], "z+", G.at[m, x, zi(k), :, B], "z-", whole=RBZ.at[m, :, 0]
            )
        elif k == 3:
            if m % 2 == 0:
                st[key] = same(G.at[m, x, zi(-3), :, B], "z+")
            else:
                st[key] = same(G.at[m, x, zi(3), :, B], "z-")
        elif k == 4:
            own = G.at[m, x, :, :, B]
            st[key] = same(own, "x+", own, "x-", whole=RB1.at[m])
        elif k == 5:
            st[key] = same(
                G.at[m, xi(-1), pl.ds(0, 4), :, B], "x+", G.at[m, xi(1), pl.ds(4, 4), :, B], "x-",
                whole=RB2.at[m],
            )

    parts = ((0, cut, RY1A, RY2A), (cut, hidden_cols - cut, RY1B, RY2B))

    def y_step(j, m, k):
        key = ("y", j, m)
        start, size, R1, R2 = parts[j]
        cols = pl.ds(start, size)
        lo, hi = pl.ds(0, half), pl.ds(half, half)
        if k > 0:
            wait2(key)
        if k == 0:
            if m == 0 and j == 0:
                load_w2.wait()
            part = jnp.dot(G[m].reshape(tok, block), W2[:, cols], preferred_element_type=F32)
            PH[m, :, :, cols] = part.astype(BF).reshape(Y, shard, size)
            st[key] = send(
                (PH.at[m, yi(2), lo, cols], R1.at[m, 0], "y+"),
                (PH.at[m, yi(2), hi, cols], R1.at[m, 1], "y-"),
                whole=R1.at[m],
            )
        elif k == 1:
            PH[m, yi(1), lo, cols] = PH[m, yi(1), lo, cols] + R1[m, 0]
            PH[m, yi(-1), hi, cols] = PH[m, yi(-1), hi, cols] + R1[m, 1]
            st[key] = send(
                (PH.at[m, yi(1), :, cols], R2.at[m, 0], "y+"),
                (PH.at[m, yi(-1), :, cols], R2.at[m, 1], "y-"),
                whole=R2.at[m],
            )
        elif k == 2:
            total = PH[m, q, :, cols].astype(F32) + R2[m, 0].astype(F32) + R2[m, 1].astype(F32)
            mine = pl.ds(pl.multiple_of(q * shard, shard), shard)
            ACT[m, q, :, cols] = jnp.where(
                H[m, mine, cols].astype(F32) > 0, total, F32(0.0)
            ).astype(BF)
            own = ACT.at[m, q, :, cols]
            st[key] = same(own, "y+", own, "y-", whole=R2.at[m])
        elif k == 3:
            st[key] = same(
                ACT.at[m, yi(-1), lo, cols], "y+", ACT.at[m, yi(1), hi, cols], "y-", whole=R1.at[m]
            )

    def norm_part(m, cols):
        part = jnp.dot(ACT[m].reshape(tok, hidden_cols), W1[:, cols], preferred_element_type=F32)
        N[m, :, :, :, cols] = part.astype(BF).reshape(X, Z, rows, cols.size)

    def mm_step(m, k):
        if m == 0:
            load_w1.wait()
        wait2(("y", 0, m))
        wait2(("y", 1, m))
        norm_part(m, pl.ds(early, block - early))

    def add(index, received):
        N[index] = N[index] + received

    def rs_a(m, k):
        key = ("rsa", m)
        if k > 0:
            wait2(key)
        lo, hi = pl.ds(0, 2), pl.ds(2, 2)
        if k == 0:
            norm_part(m, pl.ds(0, early))
            st[key] = send(
                (N.at[m, lo, zi(4), :, A], RA4.at[m, 0], "z+"),
                (N.at[m, hi, zi(4), :, A], RA4.at[m, 1], "z-"),
                whole=RA4.at[m],
            )
        elif k < 4:
            d = 4 - k
            if k == 1:
                add((m, lo, zi(3), slice(None), A), RA4[m, 0])
                add((m, hi, zi(-3), slice(None), A), RA4[m, 1])
            else:
                add((m, slice(None), zi(d), slice(None), A), RA[m, 0, d])
                add((m, slice(None), zi(-d), slice(None), A), RA[m, 1, d])
            st[key] = send(
                (N.at[m, :, zi(d), :, A], RA.at[m, 0, d - 1], "z+"),
                (N.at[m, :, zi(-d), :, A], RA.at[m, 1, d - 1], "z-"),
                whole=RA.at[m, :, d - 1],
            )
        elif k == 4:
            index = (m, slice(None), z, slice(None), A)
            N[index] = (
                N[index].astype(F32) + RA[m, 0, 0].astype(F32) + RA[m, 1, 0].astype(F32)
            ).astype(BF)
            st[key] = send((N.at[m, xi(2), z, :, A], RAX2.at[m], "x+" if m % 2 == 0 else "x-"))
        elif k == 5:
            far = xi(1) if m % 2 == 0 else xi(-1)
            add((m, far, z, slice(None), A), RAX2[m])
            st[key] = send(
                (N.at[m, xi(1), z, :, A], RAX1.at[m, 0], "x+"),
                (N.at[m, xi(-1), z, :, A], RAX1.at[m, 1], "x-"),
                whole=RAX1.at[m],
            )
        else:
            index = (m, x, z, slice(None), A)
            N[index] = (
                N[index].astype(F32) + RAX1[m, 0].astype(F32) + RAX1[m, 1].astype(F32)
            ).astype(BF)

    def rs_b(m, k):
        key = ("rsb", m)
        if k > 0:
            wait2(key)
        lo, hi = pl.ds(0, 4), pl.ds(4, 4)
        every = slice(None)
        if k == 0:
            st[key] = send(
                (N.at[m, xi(2), lo, :, B], RB2.at[m, 0], "x+"),
                (N.at[m, xi(2), hi, :, B], RB2.at[m, 1], "x-"),
                whole=RB2.at[m],
            )
        elif k == 1:
            add((m, xi(1), lo, every, B), RB2[m, 0])
            add((m, xi(-1), hi, every, B), RB2[m, 1])
            st[key] = send(
                (N.at[m, xi(1), :, :, B], RB1.at[m, 0], "x+"),
                (N.at[m, xi(-1), :, :, B], RB1.at[m, 1], "x-"),
                whole=RB1.at[m],
            )
        elif k == 2:
            index = (m, x, every, every, B)
            N[index] = (
                N[index].astype(F32) + RB1[m, 0].astype(F32) + RB1[m, 1].astype(F32)
            ).astype(BF)
            st[key] = send((N.at[m, x, zi(4), :, B], RBZ4.at[m], "z+" if m % 2 == 0 else "z-"))
        elif k < 6:
            d = 6 - k
            if k == 3:
                add((m, x, zi(3) if m % 2 == 0 else zi(-3), every, B), RBZ4[m])
            else:
                add((m, x, zi(d), every, B), RBZ[m, 0, d])
                add((m, x, zi(-d), every, B), RBZ[m, 1, d])
            st[key] = send(
                (N.at[m, x, zi(d), :, B], RBZ.at[m, 0, d - 1], "z+"),
                (N.at[m, x, zi(-d), :, B], RBZ.at[m, 1, d - 1], "z-"),
                whole=RBZ.at[m, :, d - 1],
            )
        else:
            index = (m, x, z, every, B)
            N[index] = (
                N[index].astype(F32) + RBZ[m, 0, 0].astype(F32) + RBZ[m, 1, 0].astype(F32)
            ).astype(BF)

    def weight_grad(j):
        tile = 256
        cols = pl.ds(j * tile, tile)
        left = G[:, :, :, :, cols].reshape(Y * tok, tile)
        part = lax.dot_general(
            left, H[...].reshape(Y * tok, hidden_cols), (((0,), (0,)), ((), ())),
            preferred_element_type=F32,
        )
        WGR[cols] = part.astype(BF)
        c = pltpu.make_async_copy(WGR.at[cols], wg_hbm.at[cols], lsem.at[3 + j])
        c.start()
        outs.append(c)

    outs = []

    with jax.named_scope("first"):
        for c in first:
            c.wait_recv()

    steps = {
        AG_A: ag_a, AG_B: ag_b, RS_A: rs_a, RS_B: rs_b, MM: mm_step,
        Y_LO: functools.partial(y_step, 0), Y_HI: functools.partial(y_step, 1),
    }
    for kind, m, k in ORDER:
        if kind == WG:
            weight_grad(m)
        elif kind == HF:
            hidden_step(k)
        else:
            steps[kind](m, k)

    with jax.named_scope("last"):
        last = []
        for d, where in ((1, "cy+"), (3, "cy-"), (2, "cy2"), (0, "c")):
            last += send((N.at[yi(d), x, z], final.at[q], where))
        drain()
        for c in outs:
            c.wait()
        for c in shared:
            c.wait_recv()
        for c in last:
            c.wait_recv()


STRIPS = 8


def norm_back(final, grad, layer, gain, wg_in, out, wg_out, fin, up, lay, gai, res, wg, sems):
    strips = [pl.ds(i * (wg.shape[0] // STRIPS), wg.shape[0] // STRIPS) for i in range(STRIPS)]
    ins = [pltpu.make_async_copy(wg_in.at[r], wg.at[r], sems.at[6 + i]) for i, r in enumerate(strips)]
    outs = [pltpu.make_async_copy(wg.at[r], wg_out.at[r], sems.at[6 + i]) for i, r in enumerate(strips)]
    loads = [
        pltpu.make_async_copy(src, dst, sems.at[1 + i])
        for i, (src, dst) in enumerate(((layer, lay), (final, fin), (gain, gai), (grad, up)))
    ]
    for c in loads:
        c.start()
    for c in ins:
        c.start()
    width = lay.shape[1]
    block = width // Y
    loads[0].wait()
    values = lay[...].astype(F32)
    center = values - jnp.mean(values, axis=-1, keepdims=True)
    scale = lax.rsqrt(jnp.mean(center * center, axis=-1, keepdims=True) + NORM_EPS)
    for c in loads[1:]:
        c.wait()
    for i in range(STRIPS):
        ins[i].wait()
        outs[i].start()
    total = jnp.zeros((lay.shape[0], 1), F32)
    dotted = jnp.zeros((lay.shape[0], 1), F32)
    for j in range(Y):
        cols = slice(j * block, (j + 1) * block)
        scaled = fin[j].astype(F32) * gai[:, cols]
        total += jnp.sum(scaled, axis=-1, keepdims=True)
        dotted += jnp.sum(scaled * (center[:, cols] * scale), axis=-1, keepdims=True)
    total = total / width
    dotted = dotted / width
    for j in range(Y):
        cols = slice(j * block, (j + 1) * block)
        scaled = fin[j].astype(F32) * gai[:, cols]
        bracket = scaled - total - (center[:, cols] * scale) * dotted
        res[:, cols] = (up[:, cols].astype(F32) + scale * bracket).astype(BF)
    store = pltpu.make_async_copy(res, out, sems.at[5])
    store.start()
    store.wait()
    for c in outs:
        c.wait()


SLOTS = 48
COPIES = 3 + 3 + 4 + Y * 32 + 4


def shards(grad_out, drop_seed, layer_in, ln_gain, pre_act, fc1_weight, fc2_weight):
    rows, width = grad_out.shape[2:]
    tok, hidden = pre_act.shape[2:]
    block = width // Y
    a = (block * 5 // 12) // 128 * 128
    b = block - a
    shard = tok // Y
    cut = hidden // 3
    early = block // 3
    anyspace = pl.BlockSpec(memory_space=pl.ANY)
    final, grad_there, layer_there, gain_there, weight_grad = pl.pallas_call(
        functools.partial(kernel, a, cut, early),
        out_shape=(
            jax.ShapeDtypeStruct((Y, rows, block), BF),
            jax.ShapeDtypeStruct((rows, width), BF),
            jax.ShapeDtypeStruct((rows, width), BF),
            jax.ShapeDtypeStruct((1, width), F32),
            jax.ShapeDtypeStruct((block, hidden), BF),
        ),
        in_specs=[pl.BlockSpec(memory_space=pltpu.SMEM)] + [anyspace] * 6,
        out_specs=(anyspace,) * 5,
        scratch_shapes=[
            pltpu.VMEM((rows, width), BF),
            pltpu.VMEM((Y, rows, block), BF),
            pltpu.VMEM((Y, X, Z, rows, block), BF),
            pltpu.VMEM((Y, tok, hidden), BF),
            pltpu.VMEM((hidden, block), BF),
            pltpu.VMEM((block, hidden), BF),
            pltpu.VMEM((Y, Y, shard, hidden), BF),
            pltpu.VMEM((Y, 2, shard // 2, cut), BF),
            pltpu.VMEM((Y, 2, shard, cut), BF),
            pltpu.VMEM((Y, 2, shard // 2, hidden - cut), BF),
            pltpu.VMEM((Y, 2, shard, hidden - cut), BF),
            pltpu.VMEM((Y, Y, shard, hidden), BF),
            pltpu.VMEM((Y, X, Z, rows, block), BF),
            pltpu.VMEM((Y, 2, X // 2, rows, a), BF),
            pltpu.VMEM((Y, 2, 3, X, rows, a), BF),
            pltpu.VMEM((Y, rows, a), BF),
            pltpu.VMEM((Y, 2, rows, a), BF),
            pltpu.VMEM((Y, 2, Z // 2, rows, b), BF),
            pltpu.VMEM((Y, 2, Z, rows, b), BF),
            pltpu.VMEM((Y, rows, b), BF),
            pltpu.VMEM((Y, 2, 3, rows, b), BF),
            pltpu.VMEM((block, hidden), BF),
            pltpu.SemaphoreType.DMA((SLOTS,)),
            pltpu.SemaphoreType.DMA((COPIES,)),
            pltpu.SemaphoreType.DMA((10,)),
        ],
        compiler_params=pltpu.CompilerParams(
            collective_id=0, has_side_effects=True, vmem_limit_bytes=60 * 1024 * 1024
        ),
    )(
        drop_seed, grad_out[0, 0], layer_in[0, 0], ln_gain,
        pre_act[0, 0], fc1_weight[0], fc2_weight[0],
    )
    arriving, weight_grad = pl.pallas_call(
        norm_back,
        out_shape=(
            jax.ShapeDtypeStruct((rows, width), BF),
            jax.ShapeDtypeStruct((block, hidden), BF),
        ),
        in_specs=[anyspace] * 5,
        out_specs=(anyspace,) * 2,
        scratch_shapes=[
            pltpu.VMEM((Y, rows, block), BF),
            pltpu.VMEM((rows, width), BF),
            pltpu.VMEM((rows, width), BF),
            pltpu.VMEM((1, width), F32),
            pltpu.VMEM((rows, width), BF),
            pltpu.VMEM((block, hidden), BF),
            pltpu.SemaphoreType.DMA((6 + STRIPS,)),
        ],
    )(final, grad_there, layer_there, gain_there, weight_grad)
    return (arriving[None, None], weight_grad[None])


def solution(mesh):
    placed = (
        P("section", "dp", "tensor", None),
        P("section"),
        P("section", "dp", "tensor", None),
        P("section", None),
        P("section", "dp", None, "tensor"),
        P("section", "tensor", "dp"),
        P("section", "dp", "tensor"),
    )
    return jax.shard_map(
        shards,
        mesh=mesh,
        in_specs=placed,
        out_specs=(P("section", "dp", "tensor", None), P("section", "dp", "tensor")),
        check_vma=False,
    )
```

time: 176 us -> 137 us (0.78)
  Pallas kernels: 170 us -> 136 us
  local copies, waits for them, and re-layouts: 4.84 us -> 0 us
    pallas_call x1 -> x2, Pallas kernels: 170 us -> 136 us  [the longest x1 133 us: shards(): pl.pallas_call(functools.partial(kernel, a, cut, early), out_shape=(jax.S...]
    unnamed x2 -> x0, local copies, waits for them, and re-layouts: 4.84 us -> none
where the time goes in v2:
time: 137 us
  Pallas kernels  136 us (99%)
  between operations  1.45 us (1%)
    pallas_call x1, Pallas kernels, shards(): pl.pallas_call(functools.partial(kernel, a, cut, early), out_shape=(jax.S...  133 us
    pallas_call x1, Pallas kernels, shards(): pl.pallas_call(norm_back, out_shape=(jax.ShapeDtypeStruct((rows, width),...  2.96 us

profile of v2, /device:TPU:1, one launch (start us, length us, event | category | flops | bytes accessed | tf_op | source)
XLA Modules:
  0.0 137.4 jit_solution(10523515185278590132)
XLA Ops:
  1.3 133.0 %shard_map.86 = (bf16[4,16,1536]{2,1,0:T(8,128)(2,1)}, bf16[16,6144]{1,0:T(8,128)(2,1)}, bf16[16,6144]{1,0:T(8,128)(2,1)}, f32[1,6144]{1,0:T(1,128)}, bf16[1536,768]{1,0:T(8,128)(2,1)}) custom-call(s32[1]{0:T(128)S(6)} %copy.9.seed_ref, bf16[16,6144]{1,0:T(8,128)(2,1)} %bitcast.10, bf16[16,6144]{1,0:T(8,128)(2,1)} %bitcast.11, f32[1,6144]{1,0:T(1,128)} %gain_hbm.1, ...), custom_call_target="tpu_custom_call" | custom-call | tf_op jit(solution)/shard_map/pallas_call | solution.py:485
  134.2 3.0 %shard_map.87 = (bf16[16,6144]{1,0:T(8,128)(2,1)}, bf16[1536,768]{1,0:T(8,128)(2,1)}) custom-call(bf16[4,16,1536]{2,1,0:T(8,128)(2,1)} %get-tuple-element.9.final, bf16[16,6144]{1,0:T(8,128)(2,1)} %get-tuple-element.10.grad, bf16[16,6144]{1,0:T(8,128)(2,1)} %get-tuple-element.11.layer, f32[1,6144]{1,0:T(1,128)} %get-tuple-element.12.gain, ...), custom_call_target="tpu_custom_call" | custom-call | tf_op jit(solution)/shard_map/pallas_call | solution.py:530

commit v3 on v2

--- a/solution.py
+++ b/solution.py
@@ -16,27 +16,31 @@
 AG_A, AG_B, Y_LO, RS_A, RS_B, WG, HF, Y_HI, MM = range(9)
 
 
+GATHER_DIRECT = (0,)
+SCATTER_DIRECT = (3,)
+
 ORDER = (
-    (1, 0, 0), (1, 2, 0), (0, 0, 0), (6, 0, 0), (1, 1, 0), (1, 0, 1), (0, 0, 1), (1, 2, 1), (0,
-    3, 0), (1, 1, 1), (1, 0, 2), (0, 2, 0), (0, 0, 2), (1, 0, 3), (1, 3, 0), (0, 2, 1), (1, 2,
-    2), (0, 0, 3), (0, 3, 1), (0, 2, 2), (1, 0, 4), (0, 0, 4), (0, 2, 3), (1, 2, 3), (1, 1, 2),
-    (1, 3, 1), (0, 1, 0), (0, 0, 5), (0, 3, 2), (1, 0, 5), (1, 2, 4), (1, 3, 2), (6, 0, 1), (0,
-    2, 4), (0, 1, 1), (0, 0, 6), (1, 0, 6), (2, 0, 0), (7, 0, 0), (1, 3, 3), (6, 0, 2), (2, 0,
-    1), (0, 2, 5), (1, 2, 5), (0, 3, 3), (7, 0, 1), (2, 0, 2), (1, 3, 4), (0, 3, 4), (0, 2, 6),
-    (1, 2, 6), (2, 2, 0), (7, 0, 2), (0, 1, 2), (7, 2, 0), (2, 2, 1), (0, 3, 5), (2, 0, 3), (1,
-    3, 5), (0, 1, 3), (1, 1, 3), (7, 0, 3), (7, 2, 1), (0, 3, 6), (1, 1, 4), (2, 2, 2), (1, 3,
-    6), (7, 3, 0), (2, 3, 0), (0, 1, 4), (8, 0, 4), (7, 2, 2), (4, 0, 0), (3, 0, 0), (7, 3, 1),
-    (2, 2, 3), (1, 1, 5), (7, 2, 3), (0, 1, 5), (2, 3, 1), (4, 0, 1), (3, 0, 1), (7, 3, 2), (1,
-    1, 6), (8, 2, 4), (0, 1, 6), (4, 2, 0), (3, 0, 2), (2, 3, 2), (7, 1, 0), (3, 2, 0), (7, 3,
-    3), (2, 1, 0), (2, 3, 3), (4, 0, 2), (4, 2, 1), (7, 1, 1), (2, 1, 1), (8, 3, 4), (4, 3, 0),
-    (4, 0, 3), (3, 2, 1), (3, 3, 0), (3, 0, 3), (7, 1, 2), (4, 0, 4), (2, 1, 2), (3, 2, 2), (3,
-    3, 1), (4, 3, 1), (7, 1, 3), (3, 0, 4), (2, 1, 3), (4, 2, 2), (3, 2, 3), (6, 0, 3), (8, 1,
-    4), (4, 1, 0), (3, 1, 0), (3, 3, 2), (3, 1, 1), (4, 2, 3), (4, 3, 2), (4, 1, 1), (4, 0, 5),
-    (3, 3, 3), (3, 1, 2), (6, 0, 4), (5, 1, 0), (5, 2, 0), (3, 2, 4), (4, 2, 4), (4, 3, 3), (5,
-    5, 0), (4, 1, 2), (3, 1, 3), (5, 4, 0), (3, 3, 4), (4, 1, 3), (5, 3, 0), (4, 3, 4), (3, 1,
-    4), (3, 3, 5), (3, 0, 5), (4, 0, 6), (4, 1, 4), (4, 2, 5), (5, 0, 0), (4, 3, 5), (3, 1, 5),
-    (4, 1, 5), (3, 2, 5), (4, 3, 6), (3, 0, 6), (4, 2, 6), (3, 3, 6), (3, 2, 6), (3, 1, 6), (4,
-    1, 6),
+    (6, 0, 0), (1, 2, 0), (0, 2, 0), (0, 0, 0), (1, 0, 0), (0, 2, 1), (1, 2, 1), (0, 0, 2), (0,
+    1, 0), (1, 1, 0), (0, 3, 0), (1, 3, 0), (1, 2, 2), (0, 1, 1), (0, 2, 2), (1, 3, 1), (1, 2,
+    3), (0, 0, 3), (1, 0, 4), (0, 2, 3), (1, 1, 1), (1, 2, 4), (0, 0, 4), (6, 0, 1), (0, 3, 1),
+    (0, 2, 4), (1, 0, 5), (6, 0, 3), (1, 3, 2), (0, 0, 5), (1, 2, 5), (1, 1, 2), (0, 2, 5), (0,
+    1, 2), (1, 0, 6), (0, 0, 6), (2, 0, 0), (0, 3, 2), (1, 1, 3), (7, 0, 0), (0, 2, 6), (6, 0,
+    2), (1, 2, 6), (7, 2, 0), (0, 1, 3), (2, 0, 1), (1, 3, 3), (2, 2, 0), (6, 0, 4), (7, 0, 1),
+    (5, 2, 4), (7, 2, 1), (1, 1, 4), (0, 1, 4), (2, 2, 1), (1, 3, 4), (0, 3, 3), (7, 0, 2), (2,
+    0, 2), (0, 1, 5), (0, 3, 4), (1, 1, 5), (2, 2, 2), (1, 3, 5), (7, 0, 3), (7, 2, 2), (5, 2,
+    0), (5, 2, 3), (0, 1, 6), (2, 0, 3), (1, 1, 6), (7, 1, 0), (2, 1, 0), (0, 3, 5), (5, 0, 0),
+    (7, 2, 3), (2, 2, 3), (0, 3, 6), (8, 0, 4), (4, 0, 0), (7, 1, 1), (3, 0, 0), (1, 3, 6), (7,
+    3, 0), (8, 2, 4), (4, 2, 0), (2, 1, 1), (3, 2, 0), (2, 3, 0), (4, 0, 1), (7, 1, 2), (3, 0,
+    1), (3, 2, 1), (2, 1, 2), (5, 3, 0), (7, 3, 1), (3, 0, 2), (5, 2, 2), (2, 3, 1), (4, 2, 1),
+    (5, 2, 5), (5, 1, 4), (5, 1, 1), (2, 1, 3), (3, 2, 2), (7, 1, 3), (5, 3, 3), (4, 0, 2), (7,
+    3, 2), (3, 0, 3), (5, 0, 1), (5, 0, 3), (5, 1, 2), (4, 2, 2), (2, 3, 2), (3, 2, 3), (8, 1,
+    4), (4, 1, 0), (4, 0, 3), (3, 1, 0), (5, 2, 1), (5, 0, 2), (4, 2, 3), (7, 3, 3), (2, 3, 3),
+    (3, 1, 1), (4, 1, 1), (3, 0, 4), (4, 2, 4), (4, 0, 4), (8, 3, 4), (3, 3, 0), (4, 3, 0), (3,
+    1, 2), (5, 3, 1), (4, 1, 2), (3, 3, 1), (5, 1, 5), (3, 2, 4), (5, 0, 4), (3, 1, 3), (5, 1,
+    0), (4, 3, 1), (3, 2, 5), (3, 0, 5), (4, 1, 3), (5, 0, 5), (3, 3, 2), (4, 0, 5), (5, 1, 3),
+    (4, 1, 4), (4, 2, 5), (3, 3, 3), (4, 3, 2), (5, 3, 5), (3, 1, 4), (3, 1, 5), (3, 3, 4), (3,
+    0, 6), (4, 0, 6), (4, 1, 5), (5, 3, 2), (5, 3, 4), (3, 3, 6), (3, 1, 6), (4, 2, 6), (4, 3,
+    6), (3, 2, 6), (4, 1, 6),
 )
 
 
@@ -52,7 +56,7 @@
     cols_a, cut, early, seed_ref, grad_hbm, layer_hbm, gain_hbm, pre_hbm, w1_hbm, w2_hbm,
     final, grad_out, layer_out, gain_out, wg_hbm,
     grad_ref, branch, G, H, W1, W2, PH, RY1A, RY2A, RY1B, RY2B, ACT, N, RA4, RA, RAX2, RAX1, RB2, RB1, RBZ4, RBZ,
-    WGR, ssem, rsem, lsem,
+    WACC, WGR, ssem, rsem, lsem,
 ):
     s = lax.axis_index("section")
     t = lax.axis_index("tensor")
@@ -84,11 +88,18 @@
         "y+": (s, t, yi(1)),
         "y-": (s, t, yi(-1)),
         "y2": (s, t, yi(2)),
+        "x2": (s, xi(2) * Z + z, q),
+        "z+2": (s, x * Z + zi(2), q),
+        "z-2": (s, x * Z + zi(-2), q),
+        "z+3": (s, x * Z + zi(3), q),
+        "z-3": (s, x * Z + zi(-3), q),
+        "z4": (s, x * Z + zi(4), q),
         "c": (1 - s, t, q),
         "cy+": (1 - s, t, yi(1)),
         "cy-": (1 - s, t, yi(-1)),
         "cy2": (1 - s, t, yi(2)),
     }
+    tile = 256
     count = [0]
     pending = {}
 
@@ -196,6 +207,8 @@
         if k == 0:
             own = G.at[m, x, z, :, A]
             st[key] = same(own, "x+", own, "x-", whole=RAX1.at[m])
+            if m in GATHER_DIRECT:
+                st[key] += same(own, "x2")
         elif k == 1:
             if m % 2 == 0:
                 st[key] = same(G.at[m, xi(-1), z, :, A], "x+")
@@ -216,7 +229,13 @@
         key = ("agb", m)
         if k > 0:
             wait2(key)
-        if k < 3:
+        if m in GATHER_DIRECT and k == 0:
+            own = G.at[m, x, z, :, B]
+            st[key] = same(own, "z+", own, "z-", whole=RBZ.at[m, :, 0])
+            st[key] += same(own, "z+2", own, "z-2", whole=RBZ.at[m, :, 0])
+            st[key] += same(own, "z+3", own, "z-3", whole=RBZ.at[m, :, 0])
+            st[key] += same(own, "z4")
+        elif k < 3:
             st[key] = same(
                 G.at[m, x, zi(-k), :, B], "z+", G.at[m, x, zi(k), :, B], "z-", whole=RBZ.at[m, :, 0]
             )
@@ -318,7 +337,16 @@
             N[index] = (
                 N[index].astype(F32) + RA[m, 0, 0].astype(F32) + RA[m, 1, 0].astype(F32)
             ).astype(BF)
-            st[key] = send((N.at[m, xi(2), z, :, A], RAX2.at[m], "x+" if m % 2 == 0 else "x-"))
+            if m in SCATTER_DIRECT:
+                st[key] = send(
+                    (N.at[m, xi(1), z, :, A], RAX1.at[m, 0], "x+"),
+                    (N.at[m, xi(-1), z, :, A], RAX1.at[m, 1], "x-"),
+                    whole=RAX1.at[m],
+                ) + send((N.at[m, xi(2), z, :, A], RAX2.at[m], "x2"))
+            else:
+                st[key] = send(
+                    (N.at[m, xi(2), z, :, A], RAX2.at[m], "x+" if m % 2 == 0 else "x-")
+                )
         elif k == 5:
             far = xi(1) if m % 2 == 0 else xi(-1)
             add((m, far, z, slice(None), A), RAX2[m])
@@ -329,9 +357,10 @@
             )
         else:
             index = (m, x, z, slice(None), A)
-            N[index] = (
-                N[index].astype(F32) + RAX1[m, 0].astype(F32) + RAX1[m, 1].astype(F32)
-            ).astype(BF)
+            total = N[index].astype(F32) + RAX1[m, 0].astype(F32) + RAX1[m, 1].astype(F32)
+            if m in SCATTER_DIRECT:
+                total += RAX2[m].astype(F32)
+            N[index] = total.astype(BF)
 
     def rs_b(m, k):
         key = ("rsb", m)
@@ -358,7 +387,19 @@
             N[index] = (
                 N[index].astype(F32) + RB1[m, 0].astype(F32) + RB1[m, 1].astype(F32)
             ).astype(BF)
-            st[key] = send((N.at[m, x, zi(4), :, B], RBZ4.at[m], "z+" if m % 2 == 0 else "z-"))
+            if m in SCATTER_DIRECT:
+                st[key] = ()
+                for d, up, down in ((1, "z+", "z-"), (2, "z+2", "z-2"), (3, "z+3", "z-3")):
+                    st[key] += send(
+                        (N.at[m, x, zi(d), :, B], RBZ.at[m, 0, d - 1], up),
+                        (N.at[m, x, zi(-d), :, B], RBZ.at[m, 1, d - 1], down),
+                        whole=RBZ.at[m, :, d - 1],
+                    )
+                st[key] += send((N.at[m, x, zi(4), :, B], RBZ4.at[m], "z4"))
+            else:
+                st[key] = send(
+                    (N.at[m, x, zi(4), :, B], RBZ4.at[m], "z+" if m % 2 == 0 else "z-")
+                )
         elif k < 6:
             d = 6 - k
             if k == 3:
@@ -373,22 +414,31 @@
             )
         else:
             index = (m, x, z, every, B)
-            N[index] = (
-                N[index].astype(F32) + RBZ[m, 0, 0].astype(F32) + RBZ[m, 1, 0].astype(F32)
-            ).astype(BF)
-
-    def weight_grad(j):
-        tile = 256
+            total = N[index].astype(F32) + RBZ[m, 0, 0].astype(F32) + RBZ[m, 1, 0].astype(F32)
+            if m in SCATTER_DIRECT:
+                total += RBZ4[m].astype(F32)
+                for d in (1, 2):
+                    total += RBZ[m, 0, d].astype(F32) + RBZ[m, 1, d].astype(F32)
+            N[index] = total.astype(BF)
+
+    taken = [0] * (block // tile)
+
+    def weight_grad(m, j):
         cols = pl.ds(j * tile, tile)
-        left = G[:, :, :, :, cols].reshape(Y * tok, tile)
         part = lax.dot_general(
-            left, H[...].reshape(Y * tok, hidden_cols), (((0,), (0,)), ((), ())),
+            G[m, :, :, :, cols].reshape(tok, tile), H[m], (((0,), (0,)), ((), ())),
             preferred_element_type=F32,
         )
-        WGR[cols] = part.astype(BF)
-        c = pltpu.make_async_copy(WGR.at[cols], wg_hbm.at[cols], lsem.at[3 + j])
-        c.start()
-        outs.append(c)
+        taken[j] += 1
+        if taken[j] == 1:
+            WACC[cols] = part
+        elif taken[j] < Y:
+            WACC[cols] += part
+        else:
+            WGR[cols] = (WACC[cols] + part).astype(BF)
+            c = pltpu.make_async_copy(WGR.at[cols], wg_hbm.at[cols], lsem.at[3 + j])
+            c.start()
+            outs.append(c)
 
     outs = []
 
@@ -402,7 +452,7 @@
     }
     for kind, m, k in ORDER:
         if kind == WG:
-            weight_grad(m)
+            weight_grad(m, k)
         elif kind == HF:
             hidden_step(k)
         else:
@@ -468,6 +518,7 @@
         c.wait()
 
 
+SPLIT = 768
 SLOTS = 48
 COPIES = 3 + 3 + 4 + Y * 32 + 4
 
@@ -476,7 +527,7 @@
     rows, width = grad_out.shape[2:]
     tok, hidden = pre_act.shape[2:]
     block = width // Y
-    a = (block * 5 // 12) // 128 * 128
+    a = SPLIT
     b = block - a
     shard = tok // Y
     cut = hidden // 3
@@ -515,6 +566,7 @@
             pltpu.VMEM((Y, 2, Z, rows, b), BF),
             pltpu.VMEM((Y, rows, b), BF),
             pltpu.VMEM((Y, 2, 3, rows, b), BF),
+            pltpu.VMEM((block, hidden), F32),
             pltpu.VMEM((block, hidden), BF),
             pltpu.SemaphoreType.DMA((SLOTS,)),
             pltpu.SemaphoreType.DMA((COPIES,)),

time: 137 us -> 133 us (0.971)
  Pallas kernels: 136 us -> 131 us
    pallas_call x1, Pallas kernels: 133 us -> 128 us  [shards(): pl.pallas_call(functools.partial(kernel, a, cut, early), out_shape=(jax.S...]
where the time goes in v3:
time: 133 us
  Pallas kernels  131 us (98%)
  between operations  1.45 us (1%)
    pallas_call x1, Pallas kernels, shards(): pl.pallas_call(functools.partial(kernel, a, cut, early), out_shape=(jax.S...  128 us
    pallas_call x1, Pallas kernels, shards(): pl.pallas_call(norm_back, out_shape=(jax.ShapeDtypeStruct((rows, width),...  2.96 us

profile of v3, /device:TPU:1, one launch (start us, length us, event | category | flops | bytes accessed | tf_op | source)
XLA Modules:
  0.0 132.7 jit_solution(18377154686131234994)
XLA Ops:
  1.3 128.3 %shard_map.86 = (bf16[4,16,1536]{2,1,0:T(8,128)(2,1)}, bf16[16,6144]{1,0:T(8,128)(2,1)}, bf16[16,6144]{1,0:T(8,128)(2,1)}, f32[1,6144]{1,0:T(1,128)}, bf16[1536,768]{1,0:T(8,128)(2,1)}) custom-call(s32[1]{0:T(128)S(6)} %copy.9.seed_ref, bf16[16,6144]{1,0:T(8,128)(2,1)} %bitcast.10, bf16[16,6144]{1,0:T(8,128)(2,1)} %bitcast.11, f32[1,6144]{1,0:T(1,128)} %gain_hbm.1, ...), custom_call_target="tpu_custom_call" | custom-call | tf_op jit(solution)/shard_map/pallas_call | solution.py:536
  129.6 3.0 %shard_map.87 = (bf16[16,6144]{1,0:T(8,128)(2,1)}, bf16[1536,768]{1,0:T(8,128)(2,1)}) custom-call(bf16[4,16,1536]{2,1,0:T(8,128)(2,1)} %get-tuple-element.9.final, bf16[16,6144]{1,0:T(8,128)(2,1)} %get-tuple-element.10.grad, bf16[16,6144]{1,0:T(8,128)(2,1)} %get-tuple-element.11.layer, f32[1,6144]{1,0:T(1,128)} %get-tuple-element.12.gain, ...), custom_call_target="tpu_custom_call" | custom-call | tf_op jit(solution)/shard_map/pallas_call | solution.py:582

commit v4 on v2

--- a/solution.py
+++ b/solution.py
@@ -16,27 +16,40 @@
 AG_A, AG_B, Y_LO, RS_A, RS_B, WG, HF, Y_HI, MM = range(9)
 
 
+WEIGHT_RELATIVE = True
+GATHER_FINE = (0, 1)
+SCATTER_FINE = (2, 3)
+
 ORDER = (
-    (1, 0, 0), (1, 2, 0), (0, 0, 0), (6, 0, 0), (1, 1, 0), (1, 0, 1), (0, 0, 1), (1, 2, 1), (0,
-    3, 0), (1, 1, 1), (1, 0, 2), (0, 2, 0), (0, 0, 2), (1, 0, 3), (1, 3, 0), (0, 2, 1), (1, 2,
-    2), (0, 0, 3), (0, 3, 1), (0, 2, 2), (1, 0, 4), (0, 0, 4), (0, 2, 3), (1, 2, 3), (1, 1, 2),
-    (1, 3, 1), (0, 1, 0), (0, 0, 5), (0, 3, 2), (1, 0, 5), (1, 2, 4), (1, 3, 2), (6, 0, 1), (0,
-    2, 4), (0, 1, 1), (0, 0, 6), (1, 0, 6), (2, 0, 0), (7, 0, 0), (1, 3, 3), (6, 0, 2), (2, 0,
-    1), (0, 2, 5), (1, 2, 5), (0, 3, 3), (7, 0, 1), (2, 0, 2), (1, 3, 4), (0, 3, 4), (0, 2, 6),
-    (1, 2, 6), (2, 2, 0), (7, 0, 2), (0, 1, 2), (7, 2, 0), (2, 2, 1), (0, 3, 5), (2, 0, 3), (1,
-    3, 5), (0, 1, 3), (1, 1, 3), (7, 0, 3), (7, 2, 1), (0, 3, 6), (1, 1, 4), (2, 2, 2), (1, 3,
-    6), (7, 3, 0), (2, 3, 0), (0, 1, 4), (8, 0, 4), (7, 2, 2), (4, 0, 0), (3, 0, 0), (7, 3, 1),
-    (2, 2, 3), (1, 1, 5), (7, 2, 3), (0, 1, 5), (2, 3, 1), (4, 0, 1), (3, 0, 1), (7, 3, 2), (1,
-    1, 6), (8, 2, 4), (0, 1, 6), (4, 2, 0), (3, 0, 2), (2, 3, 2), (7, 1, 0), (3, 2, 0), (7, 3,
-    3), (2, 1, 0), (2, 3, 3), (4, 0, 2), (4, 2, 1), (7, 1, 1), (2, 1, 1), (8, 3, 4), (4, 3, 0),
-    (4, 0, 3), (3, 2, 1), (3, 3, 0), (3, 0, 3), (7, 1, 2), (4, 0, 4), (2, 1, 2), (3, 2, 2), (3,
-    3, 1), (4, 3, 1), (7, 1, 3), (3, 0, 4), (2, 1, 3), (4, 2, 2), (3, 2, 3), (6, 0, 3), (8, 1,
-    4), (4, 1, 0), (3, 1, 0), (3, 3, 2), (3, 1, 1), (4, 2, 3), (4, 3, 2), (4, 1, 1), (4, 0, 5),
-    (3, 3, 3), (3, 1, 2), (6, 0, 4), (5, 1, 0), (5, 2, 0), (3, 2, 4), (4, 2, 4), (4, 3, 3), (5,
-    5, 0), (4, 1, 2), (3, 1, 3), (5, 4, 0), (3, 3, 4), (4, 1, 3), (5, 3, 0), (4, 3, 4), (3, 1,
-    4), (3, 3, 5), (3, 0, 5), (4, 0, 6), (4, 1, 4), (4, 2, 5), (5, 0, 0), (4, 3, 5), (3, 1, 5),
-    (4, 1, 5), (3, 2, 5), (4, 3, 6), (3, 0, 6), (4, 2, 6), (3, 3, 6), (3, 2, 6), (3, 1, 6), (4,
-    1, 6),
+    (6, 0, 0), (1, 0, 0), (0, 0, 0), (0, 1, 0), (1, 3, 0), (1, 1, 0), (1, 2, 0), (1, 0, 101),
+    (0, 0, 110), (0, 0, 120), (1, 1, 101), (0, 1, 120), (1, 0, 102), (0, 0, 111), (0, 2, 0), (0,
+    0, 101), (0, 0, 121), (0, 3, 0), (1, 1, 102), (1, 0, 111), (1, 0, 103), (1, 0, 110), (0, 1,
+    110), (0, 1, 101), (0, 0, 122), (0, 0, 102), (0, 0, 112), (0, 2, 1), (1, 1, 111), (1, 0,
+    104), (1, 1, 103), (0, 3, 1), (0, 1, 121), (1, 2, 1), (0, 0, 123), (0, 1, 111), (1, 0, 113),
+    (1, 0, 112), (0, 0, 103), (1, 0, 114), (0, 0, 113), (1, 3, 1), (1, 2, 2), (1, 1, 113), (6,
+    0, 1), (0, 3, 2), (1, 0, 6), (0, 1, 122), (0, 1, 112), (1, 1, 112), (0, 0, 6), (1, 1, 110),
+    (0, 1, 102), (2, 0, 0), (0, 2, 2), (1, 3, 2), (1, 1, 104), (7, 0, 0), (1, 2, 3), (1, 1,
+    114), (2, 0, 1), (0, 1, 103), (0, 1, 113), (7, 0, 1), (0, 1, 123), (1, 3, 3), (1, 1, 6), (0,
+    3, 3), (6, 0, 2), (1, 2, 4), (2, 0, 2), (0, 1, 6), (0, 2, 3), (7, 1, 0), (7, 0, 2), (1, 3,
+    4), (2, 0, 3), (0, 3, 4), (2, 1, 0), (0, 2, 4), (7, 1, 1), (7, 0, 3), (1, 2, 5), (0, 2, 5),
+    (2, 1, 1), (1, 3, 5), (7, 1, 2), (8, 0, 4), (4, 0, 0), (1, 2, 6), (2, 1, 2), (0, 2, 6), (7,
+    2, 0), (0, 3, 5), (1, 3, 6), (3, 0, 0), (7, 1, 3), (2, 2, 0), (2, 1, 3), (7, 2, 1), (3, 0,
+    1), (0, 3, 6), (5, 0, 5), (4, 0, 1), (2, 3, 0), (2, 2, 1), (7, 3, 0), (8, 1, 4), (3, 1, 0),
+    (5, 0, 1), (3, 0, 2), (7, 2, 2), (3, 1, 1), (4, 0, 2), (4, 1, 0), (2, 2, 2), (3, 0, 3), (7,
+    3, 1), (5, 0, 2), (3, 1, 2), (7, 2, 3), (4, 1, 1), (5, 3, 1), (2, 2, 3), (2, 3, 1), (5, 3,
+    0), (7, 3, 2), (4, 0, 3), (3, 1, 3), (5, 3, 3), (8, 2, 4), (4, 2, 0), (2, 3, 2), (3, 2, 0),
+    (5, 0, 0), (4, 0, 4), (5, 1, 0), (4, 1, 2), (7, 3, 3), (4, 2, 114), (3, 0, 4), (3, 2, 121),
+    (3, 2, 111), (4, 2, 113), (2, 3, 3), (3, 2, 101), (6, 0, 3), (5, 0, 3), (4, 1, 3), (4, 2,
+    104), (5, 1, 4), (3, 2, 122), (4, 2, 112), (3, 0, 5), (5, 1, 3), (4, 0, 5), (3, 2, 112), (8,
+    3, 4), (4, 1, 4), (4, 3, 0), (3, 3, 0), (4, 2, 103), (4, 0, 6), (3, 2, 113), (4, 3, 114),
+    (4, 2, 111), (3, 3, 121), (3, 3, 111), (3, 1, 4), (5, 0, 4), (4, 3, 113), (3, 3, 101), (3,
+    2, 102), (4, 3, 110), (4, 3, 104), (4, 2, 110), (3, 3, 122), (3, 2, 123), (5, 3, 4), (3, 3,
+    112), (5, 1, 1), (4, 3, 112), (3, 3, 102), (4, 3, 103), (4, 2, 102), (3, 3, 123), (6, 0, 4),
+    (3, 3, 113), (3, 1, 5), (4, 3, 111), (5, 2, 5), (5, 1, 2), (3, 2, 114), (4, 3, 102), (5, 2,
+    1), (3, 2, 103), (3, 2, 124), (4, 1, 5), (5, 3, 5), (3, 3, 103), (3, 3, 114), (4, 2, 101),
+    (3, 3, 124), (5, 2, 2), (3, 0, 6), (4, 3, 101), (5, 2, 0), (5, 2, 4), (5, 2, 3), (5, 3, 2),
+    (3, 3, 104), (3, 1, 6), (5, 1, 5), (4, 2, 6), (3, 2, 104), (4, 1, 6), (3, 2, 6), (3, 3, 6),
+    (4, 3, 6),
 )
 
 
@@ -52,7 +65,7 @@
     cols_a, cut, early, seed_ref, grad_hbm, layer_hbm, gain_hbm, pre_hbm, w1_hbm, w2_hbm,
     final, grad_out, layer_out, gain_out, wg_hbm,
     grad_ref, branch, G, H, W1, W2, PH, RY1A, RY2A, RY1B, RY2B, ACT, N, RA4, RA, RAX2, RAX1, RB2, RB1, RBZ4, RBZ,
-    WGR, ssem, rsem, lsem,
+    WACC, WGR, ssem, rsem, lsem,
 ):
     s = lax.axis_index("section")
     t = lax.axis_index("tensor")
@@ -84,11 +97,13 @@
         "y+": (s, t, yi(1)),
         "y-": (s, t, yi(-1)),
         "y2": (s, t, yi(2)),
+        "x2": (s, xi(2) * Z + z, q),
         "c": (1 - s, t, q),
         "cy+": (1 - s, t, yi(1)),
         "cy-": (1 - s, t, yi(-1)),
         "cy2": (1 - s, t, yi(2)),
     }
+    tile = 256
     count = [0]
     pending = {}
 
@@ -189,7 +204,202 @@
             return send((ref, ref, where))
         return send((ref, ref, where), (other, other, other_where), whole=whole)
 
+
+    groups = ((0,), (1, -1), (2,))
+    slot_of = {0: 0, 1: 1, -1: 2, 2: 3}
+
+    def many(parts, two, four):
+        return send(*parts, whole=(None, two, None, four)[len(parts) - 1])
+
+    def gather_a(m, k):
+        two, four = RAX1.at[m], RA4.at[m]
+
+        def on(g, d):
+            parts = []
+            for dx in groups[g]:
+                up, down = G.at[m, xi(dx), zi(-d), :, A], G.at[m, xi(dx), zi(d), :, A]
+                if d < 3 or dx in (0, 1):
+                    parts.append((up, up, "z+"))
+                if d < 3 or dx in (-1, 2):
+                    parts.append((down, down, "z-"))
+            st["ga", m, g] = many(parts, two, four)
+
+        if k == 0:
+            own = G.at[m, x, z, :, A]
+            st["gx1", m] = same(own, "x+", own, "x-", whole=two)
+            on(0, 0)
+            st["gx2", m] = same(own, "x2")
+        elif k == 6:
+            for g in range(3):
+                wait2(("ga", m, g))
+        elif k in (110, 120):
+            wait2(("gx1" if k == 110 else "gx2", m))
+            on((k - 100) // 10, 0)
+        else:
+            g = (k - 100) // 10
+            wait2(("ga", m, g))
+            on(g, k % 10)
+
+    def gather_b(m, k):
+        two, four = RBZ.at[m, :, 0], RB2.at[m, 0]
+
+        def piece(dx, dz):
+            return G.at[m, xi(dx), zi(dz), :, B]
+
+        def along_z(d):
+            parts = [(piece(0, -d), piece(0, -d), "z+")]
+            if d < 3:
+                parts.append((piece(0, d), piece(0, d), "z-"))
+            st["gz", m, d] = many(parts, two, four)
+
+        def along_x(d):
+            parts = []
+            for dz in ((d,) if d in (0, 4) else (d, -d)):
+                parts += [(piece(0, dz), piece(0, dz), w) for w in ("x+", "x-")]
+            st["gx", m, d] = many(parts, two, four)
+
+        if k == 0:
+            along_z(0)
+            along_x(0)
+        elif k == 6:
+            for d in range(5):
+                wait2(("gf", m, d))
+        elif k < 105:
+            d = k - 100
+            wait2(("gz", m, d - 1))
+            if d < 4:
+                along_z(d)
+            along_x(d)
+        else:
+            d = k - 110
+            wait2(("gx", m, d))
+            parts = []
+            if d < 4:
+                parts.append((piece(-1, d), piece(-1, d), "x+"))
+            if d > 0:
+                parts.append((piece(1, -d), piece(1, -d), "x-"))
+            st["gf", m, d] = many(parts, two, four)
+
+    def scatter_a(m, k):
+        two, four = RAX1.at[m], RA4.at[m]
+        every = slice(None)
+
+        def on(g, step):
+            parts, d = [], 4 - step
+            for dx in groups[g]:
+                i = slot_of[dx]
+                if step == 0:
+                    parts.append(
+                        (N.at[m, xi(dx), zi(4), :, A], RA4.at[m, i // 2, i % 2],
+                         "z+" if dx in (0, 1) else "z-")
+                    )
+                else:
+                    parts += [
+                        (N.at[m, xi(dx), zi(d), :, A], RA.at[m, 0, d - 1, i], "z+"),
+                        (N.at[m, xi(dx), zi(-d), :, A], RA.at[m, 1, d - 1, i], "z-"),
+                    ]
+            st["sa", m, g] = many(parts, two, four)
+
+        if k == 0:
+            norm_part(m, pl.ds(0, early))
+            for g in (2, 1, 0):
+                on(g, 0)
+        elif k == 6:
+            wait2(("sx", m, 1))
+            wait2(("sx", m, 2))
+            index = (m, x, z, every, A)
+            total = N[index].astype(F32) + RAX1[m, 0].astype(F32) + RAX1[m, 1].astype(F32)
+            N[index] = (total + RAX2[m].astype(F32)).astype(BF)
+        else:
+            g, step = (k - 100) // 10, k % 10
+            d = 4 - step
+            wait2(("sa", m, g))
+            for dx in groups[g]:
+                i = slot_of[dx]
+                if step == 1:
+                    there = zi(3) if dx in (0, 1) else zi(-3)
+                    add((m, xi(dx), there, every, A), RA4[m, i // 2, i % 2])
+                elif step < 4:
+                    add((m, xi(dx), zi(d), every, A), RA[m, 0, d, i])
+                    add((m, xi(dx), zi(-d), every, A), RA[m, 1, d, i])
+                else:
+                    index = (m, xi(dx), z, every, A)
+                    N[index] = (
+                        N[index].astype(F32) + RA[m, 0, 0, i].astype(F32) + RA[m, 1, 0, i].astype(F32)
+                    ).astype(BF)
+            if step < 4:
+                on(g, step)
+            elif g == 1:
+                st["sx", m, 1] = send(
+                    (N.at[m, xi(1), z, :, A], RAX1.at[m, 0], "x+"),
+                    (N.at[m, xi(-1), z, :, A], RAX1.at[m, 1], "x-"),
+                    whole=two,
+                )
+            elif g == 2:
+                st["sx", m, 2] = send((N.at[m, xi(2), z, :, A], RAX2.at[m], "x2"))
+
+    def scatter_b(m, k):
+        two, four = RBZ.at[m, :, 0], RB2.at[m, 0]
+        every = slice(None)
+
+        def both(d):
+            return ((d, d),) if d in (0, 4) else ((d, d), (-d, Z - d))
+
+        def summed(dz, refs):
+            index = (m, x, zi(dz), every, B)
+            total = N[index].astype(F32)
+            for ref in refs:
+                total += ref[...].astype(F32)
+            N[index] = total.astype(BF)
+
+        if k == 0:
+            for d in (4, 3, 2, 1, 0):
+                parts = []
+                if d < 4:
+                    parts.append((N.at[m, xi(2), zi(d), :, B], RB2.at[m, 0, d], "x+"))
+                if d > 0:
+                    parts.append((N.at[m, xi(2), zi(-d), :, B], RB2.at[m, 1, d - 1], "x-"))
+                st["sf", m, d] = many(parts, two, four)
+        elif k >= 110:
+            d = k - 110
+            wait2(("sf", m, d))
+            if d < 4:
+                add((m, xi(1), zi(d), every, B), RB2[m, 0, d])
+            if d > 0:
+                add((m, xi(-1), zi(-d), every, B), RB2[m, 1, d - 1])
+            parts = []
+            for dz, i in both(d):
+                parts += [
+                    (N.at[m, xi(1), zi(dz), :, B], RB1.at[m, 0, i], "x+"),
+                    (N.at[m, xi(-1), zi(dz), :, B], RB1.at[m, 1, i], "x-"),
+                ]
+            st["sn", m, d] = many(parts, two, four)
+        else:
+            d = k - 100 if k > 6 else 0
+            wait2(("sn", m, d))
+            if d < 4:
+                wait2(("sz", m, d + 1))
+            for dz, i in both(d):
+                refs = [RB1.at[m, 0, i], RB1.at[m, 1, i]]
+                if d == 3 and dz == 3:
+                    refs.append(RBZ4.at[m])
+                elif d == 0:
+                    refs += [RBZ.at[m, 0, 0], RBZ.at[m, 1, 0]]
+                elif d < 3:
+                    refs.append(RBZ.at[m, 0 if dz > 0 else 1, d])
+                summed(dz, refs)
+            if d == 4:
+                st["sz", m, 4] = send((N.at[m, x, zi(4), :, B], RBZ4.at[m], "z+"))
+            elif d > 0:
+                st["sz", m, d] = send(
+                    (N.at[m, x, zi(d), :, B], RBZ.at[m, 0, d - 1], "z+"),
+                    (N.at[m, x, zi(-d), :, B], RBZ.at[m, 1, d - 1], "z-"),
+                    whole=RBZ.at[m, :, d - 1],
+                )
+
     def ag_a(m, k):
+        if m in GATHER_FINE:
+            return gather_a(m, k)
         key = ("aga", m)
         if k > 0:
             wait2(key)
@@ -213,6 +423,8 @@
             )
 
     def ag_b(m, k):
+        if m in GATHER_FINE:
+            return gather_b(m, k)
         key = ("agb", m)
         if k > 0:
             wait2(key)
@@ -289,6 +501,8 @@
         N[index] = N[index] + received
 
     def rs_a(m, k):
+        if m in SCATTER_FINE:
+            return scatter_a(m, k)
         key = ("rsa", m)
         if k > 0:
             wait2(key)
@@ -334,6 +548,8 @@
             ).astype(BF)
 
     def rs_b(m, k):
+        if m in SCATTER_FINE:
+            return scatter_b(m, k)
         key = ("rsb", m)
         if k > 0:
             wait2(key)
@@ -377,18 +593,25 @@
                 N[index].astype(F32) + RBZ[m, 0, 0].astype(F32) + RBZ[m, 1, 0].astype(F32)
             ).astype(BF)
 
-    def weight_grad(j):
-        tile = 256
+    taken = [0] * (block // tile)
+
+    def weight_grad(m, j):
         cols = pl.ds(j * tile, tile)
-        left = G[:, :, :, :, cols].reshape(Y * tok, tile)
+        mb = yi(m) if WEIGHT_RELATIVE else m
         part = lax.dot_general(
-            left, H[...].reshape(Y * tok, hidden_cols), (((0,), (0,)), ((), ())),
+            G[mb, :, :, :, cols].reshape(tok, tile), H[mb], (((0,), (0,)), ((), ())),
             preferred_element_type=F32,
         )
-        WGR[cols] = part.astype(BF)
-        c = pltpu.make_async_copy(WGR.at[cols], wg_hbm.at[cols], lsem.at[3 + j])
-        c.start()
-        outs.append(c)
+        taken[j] += 1
+        if taken[j] == 1:
+            WACC[cols] = part
+        elif taken[j] < Y:
+            WACC[cols] += part
+        else:
+            WGR[cols] = (WACC[cols] + part).astype(BF)
+            c = pltpu.make_async_copy(WGR.at[cols], wg_hbm.at[cols], lsem.at[3 + j])
+            c.start()
+            outs.append(c)
 
     outs = []
 
@@ -402,7 +625,7 @@
     }
     for kind, m, k in ORDER:
         if kind == WG:
-            weight_grad(m)
+            weight_grad(m, k)
         elif kind == HF:
             hidden_step(k)
         else:
@@ -468,15 +691,16 @@
         c.wait()
 
 
+SPLIT = 640
 SLOTS = 48
-COPIES = 3 + 3 + 4 + Y * 32 + 4
+COPIES = 3 + 3 + 4 + Y * 32 + 4 + 16 * (len(GATHER_FINE) + len(SCATTER_FINE))
 
 
 def shards(grad_out, drop_seed, layer_in, ln_gain, pre_act, fc1_weight, fc2_weight):
     rows, width = grad_out.shape[2:]
     tok, hidden = pre_act.shape[2:]
     block = width // Y
-    a = (block * 5 // 12) // 128 * 128
+    a = SPLIT
     b = block - a
     shard = tok // Y
     cut = hidden // 3
@@ -515,6 +739,7 @@
             pltpu.VMEM((Y, 2, Z, rows, b), BF),
             pltpu.VMEM((Y, rows, b), BF),
             pltpu.VMEM((Y, 2, 3, rows, b), BF),
+            pltpu.VMEM((block, hidden), F32),
             pltpu.VMEM((block, hidden), BF),
             pltpu.SemaphoreType.DMA((SLOTS,)),
             pltpu.SemaphoreType.DMA((COPIES,)),

time: 137 us -> 128 us (0.934)
  Pallas kernels: 136 us -> 127 us
    pallas_call x1, Pallas kernels: 133 us -> 124 us  [shards(): pl.pallas_call(functools.partial(kernel, a, cut, early), out_shape=(jax.S...]
where the time goes in v4:
time: 128 us
  Pallas kernels  127 us (99%)
  between operations  1.45 us (1%)
    pallas_call x1, Pallas kernels, shards(): pl.pallas_call(functools.partial(kernel, a, cut, early), out_shape=(jax.S...  124 us
    pallas_call x1, Pallas kernels, shards(): pl.pallas_call(norm_back, out_shape=(jax.ShapeDtypeStruct((rows, width),...  2.96 us

profile of v4, /device:TPU:1, one launch (start us, length us, event | category | flops | bytes accessed | tf_op | source)
XLA Modules:
  0.0 128.1 jit_solution(11736675374725258785)
XLA Ops:
  1.3 123.7 %shard_map.86 = (bf16[4,16,1536]{2,1,0:T(8,128)(2,1)}, bf16[16,6144]{1,0:T(8,128)(2,1)}, bf16[16,6144]{1,0:T(8,128)(2,1)}, f32[1,6144]{1,0:T(1,128)}, bf16[1536,768]{1,0:T(8,128)(2,1)}) custom-call(s32[1]{0:T(128)S(6)} %copy.9.seed_ref, bf16[16,6144]{1,0:T(8,128)(2,1)} %bitcast.10, bf16[16,6144]{1,0:T(8,128)(2,1)} %bitcast.11, f32[1,6144]{1,0:T(1,128)} %gain_hbm.1, ...), custom_call_target="tpu_custom_call" | custom-call | tf_op jit(solution)/shard_map/pallas_call | solution.py:709
  125.0 3.0 %shard_map.87 = (bf16[16,6144]{1,0:T(8,128)(2,1)}, bf16[1536,768]{1,0:T(8,128)(2,1)}) custom-call(bf16[4,16,1536]{2,1,0:T(8,128)(2,1)} %get-tuple-element.9.final, bf16[16,6144]{1,0:T(8,128)(2,1)} %get-tuple-element.10.grad, bf16[16,6144]{1,0:T(8,128)(2,1)} %get-tuple-element.11.layer, f32[1,6144]{1,0:T(1,128)} %get-tuple-element.12.gain, ...), custom_call_target="tpu_custom_call" | custom-call | tf_op jit(solution)/shard_map/pallas_call | solution.py:755

commit v5 on v4

--- a/solution.py
+++ b/solution.py
@@ -65,7 +65,7 @@
     cols_a, cut, early, seed_ref, grad_hbm, layer_hbm, gain_hbm, pre_hbm, w1_hbm, w2_hbm,
     final, grad_out, layer_out, gain_out, wg_hbm,
     grad_ref, branch, G, H, W1, W2, PH, RY1A, RY2A, RY1B, RY2B, ACT, N, RA4, RA, RAX2, RAX1, RB2, RB1, RBZ4, RBZ,
-    WACC, WGR, ssem, rsem, lsem,
+    WACC, WGR, ssem, rsem, lsem, pace_sem,
 ):
     s = lax.axis_index("section")
     t = lax.axis_index("tensor")
@@ -107,17 +107,18 @@
     count = [0]
     pending = {}
 
-    def send(*parts, whole=None):
+    def send(*parts, whole=None, arrival=None):
         i = count[0]
         count[0] += 1
         slot = i % SLOTS
+        landed = i if arrival is None else arrival
         if slot in pending:
             pending.pop(slot).wait_send()
 
         def copy(src, dst, where):
             return pltpu.make_async_remote_copy(
-                src_ref=src, dst_ref=dst, send_sem=ssem.at[slot], recv_sem=rsem.at[i],
-                device_id=to[where], device_id_type=MESH,
+                src_ref=src, dst_ref=dst, send_sem=ssem.at[slot], recv_sem=rsem.at[landed],
+                device_id=to[where] if isinstance(where, str) else where, device_id_type=MESH,
             )
 
         for part in parts:
@@ -161,9 +162,23 @@
     with jax.named_scope("barrier"):
         pl.semaphore_wait(barrier, len(to))
 
-    first = []
-    for d, where in ((1, "y+"), (3, "y-"), (2, "y2")):
-        first += send((branch.at[yi(d)], G.at[q, x, z], where))
+    for d, where in ((2, "y2"), (1, "y+"), (3, "y-")):
+        send((branch.at[yi(d)], G.at[q, x, z], where), arrival=d - 1)
+    count[0] = 3
+    waited = set()
+
+    def wait_first(m):
+        if m in waited:
+            return
+        waited.add(m)
+
+        @pl.when(q != m)
+        def _():
+            pltpu.make_async_remote_copy(
+                src_ref=branch.at[0], dst_ref=branch.at[0], send_sem=ssem.at[0],
+                recv_sem=rsem.at[(q - m + Y - 1) % Y], device_id=to["y+"], device_id_type=MESH,
+            ).wait_recv()
+
     shared = []
     for src, dst in ((grad_hbm, grad_out), (layer_hbm, layer_out), (gain_hbm, gain_out)):
         shared += send((src, dst, "c"))
@@ -615,34 +630,56 @@
 
     outs = []
 
-    with jax.named_scope("first"):
-        for c in first:
-            c.wait_recv()
+    last = COPIES - 1
+    finished = []
+
+    def finish(m):
+        finished.append(m)
+        if finished.count(m) == 2:
+            send((N.at[m, x, z], final.at[q], (1 - s, t, m)), arrival=last)
 
     steps = {
         AG_A: ag_a, AG_B: ag_b, RS_A: rs_a, RS_B: rs_b, MM: mm_step,
         Y_LO: functools.partial(y_step, 0), Y_HI: functools.partial(y_step, 1),
     }
     for kind, m, k in ORDER:
+        paced = (kind, k) in PACED
+        if paced:
+
+            @pl.when(s == 1)
+            def _():
+                pl.semaphore_wait(pace_sem, 1)
+
         if kind == WG:
             weight_grad(m, k)
         elif kind == HF:
             hidden_step(k)
         else:
+            if kind in (AG_A, AG_B) and k == 0:
+                wait_first(m)
             steps[kind](m, k)
+            if kind in (RS_A, RS_B) and k == 6:
+                finish(m)
+        if paced:
+
+            @pl.when(s == 0)
+            def _():
+                pl.semaphore_signal(pace_sem, inc=1, device_id=to["c"], device_id_type=MESH)
+
 
     with jax.named_scope("last"):
-        last = []
-        for d, where in ((1, "cy+"), (3, "cy-"), (2, "cy2"), (0, "c")):
-            last += send((N.at[yi(d), x, z], final.at[q], where))
         drain()
         for c in outs:
             c.wait()
         for c in shared:
             c.wait_recv()
-        for c in last:
-            c.wait_recv()
-
+        pltpu.make_async_remote_copy(
+            src_ref=branch, dst_ref=branch, send_sem=ssem.at[0], recv_sem=rsem.at[last],
+            device_id=to["c"], device_id_type=MESH,
+        ).wait_recv()
+
+
+PACED = ((Y_LO, 0), (Y_HI, 0), (Y_HI, 1), (Y_HI, 2))
 
 STRIPS = 8
 
@@ -744,6 +781,7 @@
             pltpu.SemaphoreType.DMA((SLOTS,)),
             pltpu.SemaphoreType.DMA((COPIES,)),
             pltpu.SemaphoreType.DMA((10,)),
+            pltpu.SemaphoreType.REGULAR,
         ],
         compiler_params=pltpu.CompilerParams(
             collective_id=0, has_side_effects=True, vmem_limit_bytes=60 * 1024 * 1024

time: 128 us -> 125 us (0.977)
  Pallas kernels: 127 us -> 122 us
    pallas_call x1, Pallas kernels: 124 us -> 120 us  [shards(): pl.pallas_call(functools.partial(kernel, a, cut, early), out_shape=(jax.S...]
where the time goes in v5:
time: 125 us; the launch traced here: 124 us
  Pallas kernels  122 us (98%)
  between operations  1.45 us (1%)
    pallas_call x1, Pallas kernels, shards(): pl.pallas_call(functools.partial(kernel, a, cut, early), out_shape=(jax.S...  120 us
    pallas_call x1, Pallas kernels, shards(): pl.pallas_call(norm_back, out_shape=(jax.ShapeDtypeStruct((rows, width),...  2.96 us

profile of v5, /device:TPU:1, one launch (start us, length us, event | category | flops | bytes accessed | tf_op | source)
XLA Modules:
  0.0 123.9 jit_solution(13518059742164928957)
XLA Ops:
  1.3 119.5 %shard_map.86 = (bf16[4,16,1536]{2,1,0:T(8,128)(2,1)}, bf16[16,6144]{1,0:T(8,128)(2,1)}, bf16[16,6144]{1,0:T(8,128)(2,1)}, f32[1,6144]{1,0:T(1,128)}, bf16[1536,768]{1,0:T(8,128)(2,1)}) custom-call(s32[1]{0:T(128)S(6)} %copy.9.seed_ref, bf16[16,6144]{1,0:T(8,128)(2,1)} %bitcast.10, bf16[16,6144]{1,0:T(8,128)(2,1)} %bitcast.11, f32[1,6144]{1,0:T(1,128)} %gain_hbm.1, ...), custom_call_target="tpu_custom_call" | custom-call | tf_op jit(solution)/shard_map/pallas_call | solution.py:746
  120.8 3.0 %shard_map.87 = (bf16[16,6144]{1,0:T(8,128)(2,1)}, bf16[1536,768]{1,0:T(8,128)(2,1)}) custom-call(bf16[4,16,1536]{2,1,0:T(8,128)(2,1)} %get-tuple-element.9.final, bf16[16,6144]{1,0:T(8,128)(2,1)} %get-tuple-element.10.grad, bf16[16,6144]{1,0:T(8,128)(2,1)} %get-tuple-element.11.layer, f32[1,6144]{1,0:T(1,128)} %get-tuple-element.12.gain, ...), custom_call_target="tpu_custom_call" | custom-call | tf_op jit(solution)/shard_map/pallas_call | solution.py:793
